TPU v7x, 128 devices: a whole 4x4x4 slice. The times are simulated.
128 devices in a mesh: scan: 16 (over y_lo, x, core), obj: 8 (over z, y_hi).
Axes of the slice: x: 4, y: 4 (y_hi: 2, y_lo: 2; y = y_hi * 2 + y_lo), z: 4, core: 2. Of those that a mesh axis runs over, the one named last changes fastest.
Arguments:
- object_field: float32 [2, 1024, 2048], P(None, 'obj', 'scan'), may hold values from -6 to 6
- probe_modes: float32 [4, 256, 512], replicated, may hold values from -2 to 2
- patterns: bfloat16 [256, 256, 256], P(('scan', 'obj')), may hold values from 0.02 to 27, as said below
- gain_map: float32 [256, 256], replicated, may hold values from 0.25 to 1.75
- defect_mask: int32 [256, 256], replicated, may hold values 0 or 1
- probe_centres: int32 [256, 2], P(('scan', 'obj')), may hold values from 0 to 127
- live_counts: int32 [128], P(('scan', 'obj')), may hold values from 1 to 2, 192 in all
Outputs:
- object_field: float32 [2, 1024, 2048], P(None, 'obj', 'scan')
- step_sizes: float32 [2], replicated
- patch_energies: float32 [2, 256], P(None, ('scan', 'obj'))
Inputs may be any that keep to these rules, and one draw needn't show every extreme that they name: `patterns`: raw detector counts, positive. `live_counts`: some device has all 2 slots live.
All inputs are finite; a program needn't handle non-finite values.
Results may differ from a plain program's by a relative error of at most 0.004.
Values sent between devices are 32-bit elements; how exact they have to be, the bound alone decides.
A program may use at most 64 MiB of HBM per device.

v0:
```python
import jax
import jax.numpy as jnp
from jax import lax
from jax.sharding import PartitionSpec as P

ITERS = 2


def with_halo(block, sides, width):
    for axis, dim in sides:
        count = lax.axis_size(axis)
        forward = [(i, i + 1) for i in range(count - 1)]
        forward.append((count - 1, 0))
        backward = [(target, source) for source, target in forward]
        low = lax.ppermute(
            lax.slice_in_dim(block, block.shape[dim] - width, None, axis=dim), axis, forward
        )
        high = lax.ppermute(lax.slice_in_dim(block, 0, width, axis=dim), axis, backward)
        block = jnp.concatenate([low, block, high], axis=dim)
    return block


def transform_table(pattern_size, direction_sign):
    indices = jnp.arange(pattern_size, dtype=jnp.int32)
    phase_int = indices[:, None] * indices[None, :] % pattern_size
    angles = phase_int.astype(jnp.float32) * (2.0 * 3.141592653589793 / pattern_size)
    norm_factor = pattern_size ** (-0.5)
    real_part = jnp.cos(angles) * norm_factor
    imag_part = -direction_sign * jnp.sin(angles) * norm_factor
    upper_rows = jnp.concatenate([real_part, imag_part], axis=1)
    lower_rows = jnp.concatenate([-imag_part, real_part], axis=1)
    return jnp.concatenate([upper_rows, lower_rows], axis=0).astype(jnp.bfloat16)


def apply_table(field_data, dft_table):
    wave_shape = field_data.shape
    flat_rows = field_data.reshape(-1, wave_shape[-1])
    return jnp.dot(flat_rows, dft_table, preferred_element_type=jnp.float32).reshape(wave_shape)


def transpose_split(field_data):
    batch_count = field_data.shape[0]
    pattern_size = field_data.shape[1]
    reshaped = field_data.reshape(batch_count, pattern_size, 2, pattern_size)
    return reshaped.transpose(0, 3, 2, 1).reshape(batch_count, pattern_size, 2 * pattern_size)


def split_product(first_field, second_field):
    half_width = first_field.shape[-1] // 2
    real_a = first_field[..., :half_width]
    imag_a = first_field[..., half_width:]
    real_b = second_field[..., :half_width]
    imag_b = second_field[..., half_width:]
    return jnp.concatenate(
        [real_a * real_b - imag_a * imag_b, real_a * imag_b + imag_a * real_b], axis=-1
    )


def conjugate_split(field_data):
    half_width = field_data.shape[-1] // 2
    return jnp.concatenate([field_data[..., :half_width], -field_data[..., half_width:]], axis=-1)


def detector_amplitude(raw_counts, gain_map, defect_mask):
    corrected = raw_counts.astype(jnp.float32) * gain_map
    neighbour_mean = 0.25 * (
        jnp.roll(corrected, 1, axis=1)
        + jnp.roll(corrected, -1, axis=1)
        + jnp.roll(corrected, 1, axis=2)
        + jnp.roll(corrected, -1, axis=2)
    )
    filled = jnp.where(defect_mask[None] == 1, neighbour_mean, corrected)
    return jnp.swapaxes(jnp.sqrt(filled), 1, 2)


def exit_residual(patch_split, probe_modes, amplitude_t, forward, inverse):
    exit_wave = split_product(patch_split[:, None], probe_modes[None])
    wave_shape = exit_wave.shape
    pattern_size = wave_shape[-2]
    flat_waves = exit_wave.reshape(-1, pattern_size, 2 * pattern_size)
    half_rows = apply_table(flat_waves.astype(jnp.bfloat16), forward).astype(jnp.bfloat16)
    far_field = apply_table(transpose_split(half_rows), forward).reshape(wave_shape)
    model_power = jnp.sum(
        far_field[..., :pattern_size] ** 2 + far_field[..., pattern_size:] ** 2, axis=1
    )
    ratios = amplitude_t / jnp.sqrt(jnp.maximum(model_power, 0.25))
    revised = (far_field * jnp.concatenate([ratios, ratios], axis=-1)[:, None]).astype(jnp.bfloat16)
    back_rows = apply_table(revised.reshape(-1, pattern_size, 2 * pattern_size), inverse).astype(
        jnp.bfloat16
    )
    back_wave = apply_table(transpose_split(back_rows), inverse).reshape(wave_shape)
    residual_wave = back_wave - exit_wave
    return jnp.sum(split_product(residual_wave, conjugate_split(probe_modes)[None]), axis=1)


def fetch_object(object_field, half_width):
    return with_halo(object_field, (("scan", 2), ("obj", 1)), half_width)


def fetch_direction(direction, half_width):
    return with_halo(direction, (("scan", 2), ("obj", 1)), half_width)


def take_patches(extended, probe_centres, pattern_size):
    anchor = jnp.zeros((), jnp.int32)

    def take_single(centre_pair):
        corner = (anchor, centre_pair[0], centre_pair[1])
        return lax.dynamic_slice(extended, corner, (extended.shape[0], pattern_size, pattern_size))

    return jax.vmap(take_single)(probe_centres)


def to_split(patches):
    return jnp.concatenate([patches[:, 0], patches[:, 1]], axis=-1)


def deposit(accumulator, slot_piece, centre_pair):
    anchor = jnp.zeros((), jnp.int32)
    corner = (anchor, centre_pair[0], centre_pair[1])
    existing = lax.dynamic_slice(accumulator, corner, slot_piece.shape)
    return lax.dynamic_update_slice(accumulator, existing + slot_piece, corner)


def as_pieces(update_term, probe_power, pattern_size, alive_flag):
    planes = [
        update_term[:, :pattern_size],
        update_term[:, pattern_size:],
        probe_power * alive_flag,
    ]
    return jnp.stack(planes)


def fold_edges(padded, axis_number, tile_size, half_width):
    interior = lax.slice_in_dim(
        padded, 2 * half_width, 2 * half_width + tile_size, axis=axis_number
    )
    leading = lax.slice_in_dim(padded, 0, half_width, axis=axis_number)
    trailing = lax.slice_in_dim(
        padded, tile_size + 3 * half_width, tile_size + 4 * half_width, axis=axis_number
    )
    return interior + leading + trailing


def on_device(
    object_field, probe_modes, patterns, gain_map, defect_mask, probe_centres, live_counts
):
    pattern_size = probe_modes.shape[1]
    half_width = pattern_size // 2
    tile_size = object_field.shape[1]
    forward = transform_table(pattern_size, 1.0)
    inverse = transform_table(pattern_size, -1.0)
    amplitude_t = detector_amplitude(patterns, gain_map, defect_mask)
    slot_count = patterns.shape[0]
    live_number = live_counts[0]
    alive_flags = (jnp.arange(slot_count, dtype=jnp.int32) < live_number).astype(jnp.float32)
    probe_power = jnp.sum(
        probe_modes[..., :pattern_size] ** 2 + probe_modes[..., pattern_size:] ** 2, axis=0
    )
    extent = tile_size + pattern_size
    step_list = []
    energy_list = []
    extended = object_field
    for iteration in range(ITERS):
        extended = fetch_object(object_field, half_width)
        zero_field = jnp.zeros((3, extent, extent), jnp.float32)
        patches = to_split(take_patches(extended, probe_centres, pattern_size))
        updates = exit_residual(patches, probe_modes, amplitude_t, forward, inverse)

        def add_slot(slot_index, accumulator):
            alive_flag = alive_flags[slot_index]
            slot_piece = as_pieces(
                updates[slot_index] * alive_flag, probe_power, pattern_size, alive_flag
            )
            return deposit(accumulator, slot_piece, probe_centres[slot_index])

        accumulator = lax.fori_loop(0, slot_count, add_slot, zero_field)
        padded = with_halo(accumulator, (("scan", 2), ("obj", 1)), half_width)
        folded = fold_edges(fold_edges(padded, 1, tile_size, half_width), 2, tile_size, half_width)
        gradient = folded[:2]
        cover_plane = folded[2]
        direction = gradient / (cover_plane + 0.5)[None]
        numerator = jnp.sum(direction * gradient)
        direction_ext = fetch_direction(direction, half_width)
        direction_patches = take_patches(direction_ext, probe_centres, pattern_size)
        patch_energy = jnp.sum(
            probe_power[None] * jnp.sum(direction_patches * direction_patches, axis=1), axis=(1, 2)
        )
        slot_energy = alive_flags * patch_energy
        denominator = jnp.sum(slot_energy)
        global_sums = lax.psum((numerator, denominator, jnp.sum(alive_flags)), ("scan", "obj"))
        step_size = global_sums[0] / global_sums[1]
        step_list.append(step_size)
        energy_list.append(slot_energy * (global_sums[2] / global_sums[1]))
        object_field = object_field + step_size * direction
    return (object_field, jnp.stack(step_list), jnp.stack(energy_list))


def solution(mesh):
    placed = (
        P(None, "obj", "scan"),
        P(),
        P(("scan", "obj"), None, None),
        P(),
        P(),
        P(("scan", "obj"), None),
        P(("scan", "obj")),
    )
    return jax.shard_map(
        on_device,
        mesh=mesh,
        in_specs=placed,
        out_specs=(P(None, "obj", "scan"), P(), P(None, ("scan", "obj"))),
        check_vma=False,
    )
```

profile of v0, /device:TPU:1, one launch (start us, length us, event | category | flops | bytes accessed | tf_op | source)
XLA Modules:
  0.0 563.6 jit_solution(11479241171709653972)
XLA Ops:
  22.2 3.0 collective-permute-start.2
  25.2 4.1 collective-permute-start.3
  29.3 3.1 slice_bitcast_fusion.5
  32.3 3.0 collective-permute-done.2
  35.3 6.1 %collective-permute-done.3 = f32[2,128,384]{2,1,0:T(8,128)S(1)} collective-permute-done((f32[2,128,384]{2,1,0:T(8,128)S(1)}, f32[2,128,384]{2,1,0:T(8,128)S(1)}, u32[]{:S(2)}, u32[]{:S(2)}) %collective-permute-start.3) | collective-permute-done | bytes 393248 | tf_op jit(solution)/shard_map/ppermute | solution.py:18
  42.6 5.9 %while.32 = (s32[]{:T(128)}, f32[2,384,384]{2,1,0:T(8,128)S(1)}, s32[2,3]{1,0:T(2,128)S(1)}, f32[2,2,256,256]{3,2,1,0:T(8,128)}, s32[]{:T(128)}) while((s32[]{:T(128)}, f32[2,384,384]{2,1,0:T(8,128)S(1)}, s32[2,3]{1,0:T(2,128)S(1)}, f32[2,2,256,256]{3,2,1,0:T(8,128)}, s32[]{:T(128)}) %tuple.154), condition=%wide.while_cond, body=%wide.while_body.sunk | while | flops 2 | bytes 1050217 | solution.py:109
  58.8 6.4 %copy.35 = bf16[8,256,2,256]{3,2,1,0:T(2,128)(2,1)} copy(bf16[8,256,2,256]{1,2,3,0:T(2,128)(2,1)S(1)} %bitcast.174) | data formatting | bytes 4194304 | tf_op jit(solution)/shard_map/transpose | solution.py:45
  65.2 3.2 dot_general.37
  77.1 6.4 %copy.37 = bf16[8,256,2,256]{3,2,1,0:T(2,128)(2,1)} copy(bf16[8,256,2,256]{1,2,3,0:T(2,128)(2,1)S(1)} %bitcast.175) | data formatting | bytes 4194304 | tf_op jit(solution)/shard_map/transpose | solution.py:45
  83.6 3.2 dot_general.41
  86.8 3.7 maximum_subtract_fusion
  92.4 38.8 %while.30 = (s32[]{:T(128)}, f32[3,384,384]{2,1,0:T(8,128)S(1)}, s32[2,2]{1,0:T(2,128)S(1)}, f32[2,256,512]{2,1,0:T(8,128)}, f32[2]{0:T(128)S(1)}, /*index=5*/f3...) while((s32[]{:T(128)}, f32[3,384,384]{2,1,0:T(8,128)S(1)}, s32[2,2]{1,0:T(2,128)S(1)}, ...), condition=%wide.region_4.5_spmd, body=%wide.region_3.4_spmd.sunk | while | flops 786440 | bytes 6553833 | solution.py:177
  100.2 11.9 %dynamic_update_slice.16 = f32[3,384,384]{2,1,0:T(8,128)S(1)} dynamic-update-slice(f32[3,384,384]{2,1,0:T(8,128)S(1)} %get-tuple-element.622, f32[3,256,256]{2,1,0:T(8,128)S(1)} %maximum_add_fusion.5, s32[]{:T(128)} %constant.86.clone.1..sunk, s32[]{:T(128)S(6)} %select_n.117, s32[]{:T(128)S(6)} %select_n.118) | dynamic-update-slice | bytes 1572868 | tf_op jit(solution)/shard_map/while/body/eval_jaxpr/dynamic_update_slice | solution.py:122
  119.9 11.3 %dynamic_update_slice.16 = f32[3,384,384]{2,1,0:T(8,128)S(1)} dynamic-update-slice(f32[3,384,384]{2,1,0:T(8,128)S(1)} %get-tuple-element.622, f32[3,256,256]{2,1,0:T(8,128)S(1)} %maximum_add_fusion.5, s32[]{:T(128)} %constant.86.clone.1..sunk, s32[]{:T(128)S(6)} %select_n.117, s32[]{:T(128)S(6)} %select_n.118) | dynamic-update-slice | bytes 1572868 | tf_op jit(solution)/shard_map/while/body/eval_jaxpr/dynamic_update_slice | solution.py:122
  131.4 3.1 collective-permute-start.4
  134.4 6.8 %collective-permute-done.4 = f32[3,384,128]{2,1,0:T(8,128)S(1)} collective-permute-done((f32[3,384,128]{2,1,0:T(8,128)S(1)}, f32[3,384,128]{2,1,0:T(8,128)S(1)}, u32[]{:S(2)}, u32[]{:S(2)}) %collective-permute-start.4) | collective-permute-done | bytes 589856 | tf_op jit(solution)/shard_map/ppermute | solution.py:15
  144.2 3.0 collective-permute-start.6
  149.6 20.6 %collective-permute-done.6 = f32[3,128,640]{2,1,0:T(8,128)S(1)} collective-permute-done((f32[3,128,640]{2,1,0:T(8,128)S(1)}, f32[3,128,640]{2,1,0:T(8,128)S(1)}, u32[]{:S(2)}, u32[]{:S(2)}) %collective-permute-start.6) | collective-permute-done | bytes 983072 | tf_op jit(solution)/shard_map/ppermute | solution.py:15
  170.2 22.8 %collective-permute-done.7 = f32[3,128,640]{2,1,0:T(8,128)S(1)} collective-permute-done((f32[3,128,640]{2,1,0:T(8,128)S(1)}, f32[3,128,640]{2,1,0:T(8,128)S(1)}, u32[]{:S(2)}, u32[]{:S(2)}) %collective-permute-start.7) | collective-permute-done | bytes 983072 | tf_op jit(solution)/shard_map/ppermute | solution.py:18
  198.8 3.3 collective-permute-start.10
  203.9 6.9 %collective-permute-done.10 = f32[2,128,384]{2,1,0:T(8,128)S(1)} collective-permute-done((f32[2,128,384]{2,1,0:T(8,128)S(1)}, f32[2,128,384]{2,1,0:T(8,128)S(1)}, u32[]{:S(2)}, u32[]{:S(2)}) %collective-permute-start.10) | collective-permute-done | bytes 393248 | tf_op jit(solution)/shard_map/ppermute | solution.py:15
  210.8 8.5 %collective-permute-done.11 = f32[2,128,384]{2,1,0:T(8,128)S(1)} collective-permute-done((f32[2,128,384]{2,1,0:T(8,128)S(1)}, f32[2,128,384]{2,1,0:T(8,128)S(1)}, u32[]{:S(2)}, u32[]{:S(2)}) %collective-permute-start.11) | collective-permute-done | bytes 393248 | tf_op jit(solution)/shard_map/ppermute | solution.py:18
  219.5 4.4 while.33
  224.8 65.8 %all-reduce.1 = (f32[]{:T(128)}, f32[]{:T(128)}) all-reduce(f32[]{:T(128)} %get-tuple-element.322, f32[]{:T(128)} %select_reduce_fusion.1), channel_id=1, replica_groups=mesh['scan'=16,'obj'=8] {'scan','obj'}, use_global_device_ids=true, to_apply=%region_6.7 | all-reduce | flops 2 | bytes 16 | tf_op jit(solution)/shard_map/psum | solution.py:191
  295.0 2.7 collective-permute-done.13
  298.7 4.4 collective-permute-start.15
  303.1 7.5 %collective-permute-done.14 = f32[2,128,384]{2,1,0:T(8,128)S(1)} collective-permute-done((f32[2,128,384]{2,1,0:T(8,128)S(1)}, f32[2,128,384]{2,1,0:T(8,128)S(1)}, u32[]{:S(2)}, u32[]{:S(2)}) %collective-permute-start.14) | collective-permute-done | bytes 393248 | tf_op jit(solution)/shard_map/ppermute | solution.py:15
  310.6 4.7 collective-permute-done.15
  315.6 4.4 while.34
  329.4 6.4 %copy.39 = bf16[8,256,2,256]{3,2,1,0:T(2,128)(2,1)} copy(bf16[8,256,2,256]{1,2,3,0:T(2,128)(2,1)S(1)} %bitcast.176) | data formatting | bytes 4194304 | tf_op jit(solution)/shard_map/transpose | solution.py:45
  335.8 3.2 dot_general.44
  347.0 6.4 %copy.40 = bf16[8,256,2,256]{3,2,1,0:T(2,128)(2,1)} copy(bf16[8,256,2,256]{1,2,3,0:T(2,128)(2,1)S(1)} %bitcast.177) | data formatting | bytes 4194304 | tf_op jit(solution)/shard_map/transpose | solution.py:45
  353.5 3.2 dot_general.48
  356.6 3.7 maximum_subtract_fusion.1
  362.3 38.7 %while.31 = (s32[]{:T(128)}, f32[3,384,384]{2,1,0:T(8,128)S(1)}, s32[2,2]{1,0:T(2,128)S(1)}, f32[2,256,512]{2,1,0:T(8,128)}, f32[2]{0:T(128)S(1)}, /*index=5*/f3...) while((s32[]{:T(128)}, f32[3,384,384]{2,1,0:T(8,128)S(1)}, s32[2,2]{1,0:T(2,128)S(1)}, ...), condition=%wide.region_14.15_spmd, body=%wide.region_13.14_spmd.sunk | while | flops 786440 | bytes 6553833 | solution.py:177
  370.0 11.9 %dynamic_update_slice.17 = f32[3,384,384]{2,1,0:T(8,128)S(1)} dynamic-update-slice(f32[3,384,384]{2,1,0:T(8,128)S(1)} %get-tuple-element.679, f32[3,256,256]{2,1,0:T(8,128)S(1)} %maximum_add_fusion.6, s32[]{:T(128)} %constant.86.clone.1..sunk.1, s32[]{:T(128)S(6)} %select_n.119, s32[]{:T(128)S(6)} %select_n.120) | dynamic-update-slice | bytes 1572868 | tf_op jit(solution)/shard_map/while/body/eval_jaxpr/dynamic_update_slice | solution.py:122
  389.7 11.3 %dynamic_update_slice.17 = f32[3,384,384]{2,1,0:T(8,128)S(1)} dynamic-update-slice(f32[3,384,384]{2,1,0:T(8,128)S(1)} %get-tuple-element.679, f32[3,256,256]{2,1,0:T(8,128)S(1)} %maximum_add_fusion.6, s32[]{:T(128)} %constant.86.clone.1..sunk.1, s32[]{:T(128)S(6)} %select_n.119, s32[]{:T(128)S(6)} %select_n.120) | dynamic-update-slice | bytes 1572868 | tf_op jit(solution)/shard_map/while/body/eval_jaxpr/dynamic_update_slice | solution.py:122
  402.6 6.8 %collective-permute-done.16 = f32[3,384,128]{2,1,0:T(8,128)S(1)} collective-permute-done((f32[3,384,128]{2,1,0:T(8,128)S(1)}, f32[3,384,128]{2,1,0:T(8,128)S(1)}, u32[]{:S(2)}, u32[]{:S(2)}) %collective-permute-start.16) | collective-permute-done | bytes 589856 | tf_op jit(solution)/shard_map/ppermute | solution.py:15
  409.5 3.0 collective-permute-done.17
  414.7 3.4 collective-permute-start.19
  418.1 19.8 %collective-permute-done.18 = f32[3,128,640]{2,1,0:T(8,128)S(1)} collective-permute-done((f32[3,128,640]{2,1,0:T(8,128)S(1)}, f32[3,128,640]{2,1,0:T(8,128)S(1)}, u32[]{:S(2)}, u32[]{:S(2)}) %collective-permute-start.18) | collective-permute-done | bytes 983072 | tf_op jit(solution)/shard_map/ppermute | solution.py:15
  437.8 22.3 %collective-permute-done.19 = f32[3,128,640]{2,1,0:T(8,128)S(1)} collective-permute-done((f32[3,128,640]{2,1,0:T(8,128)S(1)}, f32[3,128,640]{2,1,0:T(8,128)S(1)}, u32[]{:S(2)}, u32[]{:S(2)}) %collective-permute-start.19) | collective-permute-done | bytes 983072 | tf_op jit(solution)/shard_map/ppermute | solution.py:18
  464.6 2.7 collective-permute-done.21
  467.6 5.0 collective-permute-start.23
  473.1 7.0 %collective-permute-done.22 = f32[2,128,384]{2,1,0:T(8,128)S(1)} collective-permute-done((f32[2,128,384]{2,1,0:T(8,128)S(1)}, f32[2,128,384]{2,1,0:T(8,128)S(1)}, u32[]{:S(2)}, u32[]{:S(2)}) %collective-permute-start.22) | collective-permute-done | bytes 393248 | tf_op jit(solution)/shard_map/ppermute | solution.py:15
  480.1 5.0 collective-permute-done.23
  485.3 4.4 while.35
  490.6 66.9 %all-reduce = (f32[]{:T(128)}, f32[]{:T(128)}, f32[]{:T(128)}) all-reduce(f32[]{:T(128)} %get-tuple-element.316, f32[]{:T(128)} %select_reduce_fusion, f32[]{:T(128)} %fusion.51), channel_id=1, replica_groups=mesh['scan'=16,'obj'=8] {'scan','obj'}, use_global_device_ids=true, to_apply=%region_16.17 | all-reduce | flops 3 | bytes 24 | tf_op jit(solution)/shard_map/psum | solution.py:191
  (234 shorter events, 127.0 us)
Async XLA Ops:
  0.6 19.7 %collective-permute-start = (f32[2,128,128]{2,1,0:T(8,128)}, f32[2,128,128]{2,1,0:T(8,128)}, u32[]{:S(2)}, u32[]{:S(2)}) collective-permute-start(f32[2,128,128]{2,1,0:T(8,128)} %param.11), channel_id=1, source_target_pairs={{0,8},{8,16},{16,24},{24,32},{32,40},{40,48},{48,56},{56,64},{64,7... | collective-permute-start | bytes 393224 | tf_op jit(solution)/shard_map/ppermute | solution.py:15
  3.3 18.0 %collective-permute-start.1 = (f32[2,128,128]{2,1,0:T(8,128)}, f32[2,128,128]{2,1,0:T(8,128)}, u32[]{:S(2)}, u32[]{:S(2)}) collective-permute-start(f32[2,128,128]{2,1,0:T(8,128)} %param.11), channel_id=1, source_target_pairs={{8,0},{16,8},{24,16},{32,24},{40,32},{48,40},{56,48},{64,56},{72,6... | collective-permute-start | bytes 393224 | tf_op jit(solution)/shard_map/ppermute | solution.py:18
  8.7 1.9 copy-start.32
  8.7 2.0 copy-start.8
  13.3 37.6 %copy-start = (f32[4,256,256]{2,1,0:T(8,128)}, f32[4,256,256]{2,1,0:T(8,128)S(1)}, u32[]{:S(2)}) copy-start(f32[4,256,256]{2,1,0:T(8,128)S(1)} %get-tuple-element.363) | copy-start | bytes 3145732
  13.3 37.6 %copy-start.2 = (f32[4,256,256]{2,1,0:T(8,128)}, f32[4,256,256]{2,1,0:T(8,128)S(1)}, u32[]{:S(2)}) copy-start(f32[4,256,256]{2,1,0:T(8,128)S(1)} %get-tuple-element.364) | copy-start | bytes 3145732
  13.3 1.7 copy-start.14
  13.3 2.0 copy-start.15
  13.3 2.5 copy-start.16
  13.3 2.8 copy-start.25
  13.3 2.9 copy-start.26
  13.4 3.0 copy-start.27
  13.4 3.1 copy-start.28
  16.4 4.8 copy-start.29
  22.2 13.1 %collective-permute-start.2 = (f32[2,128,384]{2,1,0:T(8,128)S(1)}, f32[2,128,384]{2,1,0:T(8,128)S(1)}, u32[]{:S(2)}, u32[]{:S(2)}) collective-permute-start(f32[2,128,384]{2,1,0:T(8,128)S(1)} %constant_dynamic-update-slice_fusion), channel_id=1, source_target_pairs={{0,1},{1,2},{2,3},{3,4},{4,5},{5,6},{6,7},{7,0},{8,9},{9,10},{10,1... | collective-permute-start | bytes 1179656 | tf_op jit(solution)/shard_map/ppermute | solution.py:15
  25.2 16.2 %collective-permute-start.3 = (f32[2,128,384]{2,1,0:T(8,128)S(1)}, f32[2,128,384]{2,1,0:T(8,128)S(1)}, u32[]{:S(2)}, u32[]{:S(2)}) collective-permute-start(f32[2,128,384]{2,1,0:T(8,128)S(1)} %constant_dynamic-update-slice_fusion), channel_id=1, source_target_pairs={{1,0},{2,1},{3,2},{4,3},{5,4},{6,5},{7,6},{0,7},{9,8},{10,9},{11,1... | collective-permute-start | bytes 1179656 | tf_op jit(solution)/shard_map/ppermute | solution.py:18
  50.9 2.7 copy-start.11
  50.9 2.7 copy-start.21
  50.9 2.7 copy-start.23
  86.7 3.7 copy-start.4
  86.7 3.7 copy-start.6
  131.4 9.9 %collective-permute-start.4 = (f32[3,384,128]{2,1,0:T(8,128)S(1)}, f32[3,384,128]{2,1,0:T(8,128)S(1)}, u32[]{:S(2)}, u32[]{:S(2)}) collective-permute-start(f32[3,384,128]{2,1,0:T(8,128)S(1)} %get-tuple-element.368), channel_id=1, source_target_pairs={{0,8},{8,16},{16,24},{24,32},{32,40},{40,48},{48,56},{56,64},{64,7... | collective-permute-start | bytes 1769480 | tf_op jit(solution)/shard_map/ppermute | solution.py:15
  134.4 9.6 %collective-permute-start.5 = (f32[3,384,128]{2,1,0:T(8,128)S(1)}, f32[3,384,128]{2,1,0:T(8,128)S(1)}, u32[]{:S(2)}, u32[]{:S(2)}) collective-permute-start(f32[3,384,128]{2,1,0:T(8,128)S(1)} %get-tuple-element.367), channel_id=1, source_target_pairs={{8,0},{16,8},{24,16},{32,24},{40,32},{48,40},{56,48},{64,56},{72,6... | collective-permute-start | bytes 1769480 | tf_op jit(solution)/shard_map/ppermute | solution.py:18
  144.2 25.9 %collective-permute-start.6 = (f32[3,128,640]{2,1,0:T(8,128)S(1)}, f32[3,128,640]{2,1,0:T(8,128)S(1)}, u32[]{:S(2)}, u32[]{:S(2)}) collective-permute-start(f32[3,128,640]{2,1,0:T(8,128)S(1)} %get-tuple-element.356), channel_id=1, source_target_pairs={{0,1},{1,2},{2,3},{3,4},{4,5},{5,6},{6,7},{7,0},{8,9},{9,10},{10,1... | collective-permute-start | bytes 2949128 | tf_op jit(solution)/shard_map/ppermute | solution.py:15
  147.2 45.8 %collective-permute-start.7 = (f32[3,128,640]{2,1,0:T(8,128)S(1)}, f32[3,128,640]{2,1,0:T(8,128)S(1)}, u32[]{:S(2)}, u32[]{:S(2)}) collective-permute-start(f32[3,128,640]{2,1,0:T(8,128)S(1)} %get-tuple-element.357), channel_id=1, source_target_pairs={{1,0},{2,1},{3,2},{4,3},{5,4},{6,5},{7,6},{0,7},{9,8},{10,9},{11,1... | collective-permute-start | bytes 2949128 | tf_op jit(solution)/shard_map/ppermute | solution.py:18
  193.8 2.4 collective-permute-start.8
  194.3 4.4 collective-permute-start.9
  198.8 12.0 %collective-permute-start.10 = (f32[2,128,384]{2,1,0:T(8,128)S(1)}, f32[2,128,384]{2,1,0:T(8,128)S(1)}, u32[]{:S(2)}, u32[]{:S(2)}) collective-permute-start(f32[2,128,384]{2,1,0:T(8,128)S(1)} %pad_maximum_fusion.10), channel_id=1, source_target_pairs={{0,1},{1,2},{2,3},{3,4},{4,5},{5,6},{6,7},{7,0},{8,9},{9,10},{10,1... | collective-permute-start | bytes 1179656 | tf_op jit(solution)/shard_map/ppermute | solution.py:15
  202.0 17.3 %collective-permute-start.11 = (f32[2,128,384]{2,1,0:T(8,128)S(1)}, f32[2,128,384]{2,1,0:T(8,128)S(1)}, u32[]{:S(2)}, u32[]{:S(2)}) collective-permute-start(f32[2,128,384]{2,1,0:T(8,128)S(1)} %pad_maximum_fusion.10), channel_id=1, source_target_pairs={{1,0},{2,1},{3,2},{4,3},{5,4},{6,5},{7,6},{0,7},{9,8},{10,9},{11,1... | collective-permute-start | bytes 1179656 | tf_op jit(solution)/shard_map/ppermute | solution.py:18
  223.8 68.1 %copy-start.30 = (f32[2,128,128]{2,1,0:T(8,128)S(1)}, f32[2,128,128]{2,1,0:T(8,128)}, u32[]{:S(2)}) copy-start(f32[2,128,128]{2,1,0:T(8,128)} %param.11) | copy-start | bytes 393220
  291.9 23.6 %copy-start.12 = (f32[2,128,128]{2,1,0:T(8,128)}, f32[2,128,128]{2,1,0:T(8,128)S(1)}, u32[]{:S(2)}) copy-start(f32[2,128,128]{2,1,0:T(8,128)S(1)} %multiply_add_fusion.5) | copy-start | bytes 393220
  292.0 3.0 collective-permute-start.12
  293.1 4.7 collective-permute-start.13
  297.8 12.9 %collective-permute-start.14 = (f32[2,128,384]{2,1,0:T(8,128)S(1)}, f32[2,128,384]{2,1,0:T(8,128)S(1)}, u32[]{:S(2)}, u32[]{:S(2)}) collective-permute-start(f32[2,128,384]{2,1,0:T(8,128)S(1)} %pad_maximum_fusion.11), channel_id=1, source_target_pairs={{0,1},{1,2},{2,3},{3,4},{4,5},{5,6},{6,7},{7,0},{8,9},{9,10},{10,1... | collective-permute-start | bytes 1179656 | tf_op jit(solution)/shard_map/ppermute | solution.py:15
  298.7 16.7 %collective-permute-start.15 = (f32[2,128,384]{2,1,0:T(8,128)S(1)}, f32[2,128,384]{2,1,0:T(8,128)S(1)}, u32[]{:S(2)}, u32[]{:S(2)}) collective-permute-start(f32[2,128,384]{2,1,0:T(8,128)S(1)} %pad_maximum_fusion.11), channel_id=1, source_target_pairs={{1,0},{2,1},{3,2},{4,3},{5,4},{6,5},{7,6},{0,7},{9,8},{10,9},{11,1... | collective-permute-start | bytes 1179656 | tf_op jit(solution)/shard_map/ppermute | solution.py:18
  321.5 2.7 copy-start.22
  321.5 2.7 copy-start.24
  356.6 3.7 copy-start.5
  356.6 3.7 copy-start.7
  401.1 8.3 %collective-permute-start.16 = (f32[3,384,128]{2,1,0:T(8,128)S(1)}, f32[3,384,128]{2,1,0:T(8,128)S(1)}, u32[]{:S(2)}, u32[]{:S(2)}) collective-permute-start(f32[3,384,128]{2,1,0:T(8,128)S(1)} %get-tuple-element.366), channel_id=1, source_target_pairs={{0,8},{8,16},{16,24},{24,32},{32,40},{40,48},{48,56},{56,64},{64,7... | collective-permute-start | bytes 1769480 | tf_op jit(solution)/shard_map/ppermute | solution.py:15
  402.5 10.0 %collective-permute-start.17 = (f32[3,384,128]{2,1,0:T(8,128)S(1)}, f32[3,384,128]{2,1,0:T(8,128)S(1)}, u32[]{:S(2)}, u32[]{:S(2)}) collective-permute-start(f32[3,384,128]{2,1,0:T(8,128)S(1)} %get-tuple-element.365), channel_id=1, source_target_pairs={{8,0},{16,8},{24,16},{32,24},{40,32},{48,40},{56,48},{64,56},{72,6... | collective-permute-start | bytes 1769480 | tf_op jit(solution)/shard_map/ppermute | solution.py:18
  412.7 25.1 %collective-permute-start.18 = (f32[3,128,640]{2,1,0:T(8,128)S(1)}, f32[3,128,640]{2,1,0:T(8,128)S(1)}, u32[]{:S(2)}, u32[]{:S(2)}) collective-permute-start(f32[3,128,640]{2,1,0:T(8,128)S(1)} %get-tuple-element.354), channel_id=1, source_target_pairs={{0,1},{1,2},{2,3},{3,4},{4,5},{5,6},{6,7},{7,0},{8,9},{9,10},{10,1... | collective-permute-start | bytes 2949128 | tf_op jit(solution)/shard_map/ppermute | solution.py:15
  414.7 45.5 %collective-permute-start.19 = (f32[3,128,640]{2,1,0:T(8,128)S(1)}, f32[3,128,640]{2,1,0:T(8,128)S(1)}, u32[]{:S(2)}, u32[]{:S(2)}) collective-permute-start(f32[3,128,640]{2,1,0:T(8,128)S(1)} %get-tuple-element.355), channel_id=1, source_target_pairs={{1,0},{2,1},{3,2},{4,3},{5,4},{6,5},{7,6},{0,7},{9,8},{10,9},{11,1... | collective-permute-start | bytes 2949128 | tf_op jit(solution)/shard_map/ppermute | solution.py:18
  461.0 3.6 collective-permute-start.20
  462.7 4.7 collective-permute-start.21
  467.4 12.7 %collective-permute-start.22 = (f32[2,128,384]{2,1,0:T(8,128)S(1)}, f32[2,128,384]{2,1,0:T(8,128)S(1)}, u32[]{:S(2)}, u32[]{:S(2)}) collective-permute-start(f32[2,128,384]{2,1,0:T(8,128)S(1)} %pad_maximum_fusion.12), channel_id=1, source_target_pairs={{0,1},{1,2},{2,3},{3,4},{4,5},{5,6},{6,7},{7,0},{8,9},{9,10},{10,1... | collective-permute-start | bytes 1179656 | tf_op jit(solution)/shard_map/ppermute | solution.py:15
  467.6 17.6 %collective-permute-start.23 = (f32[2,128,384]{2,1,0:T(8,128)S(1)}, f32[2,128,384]{2,1,0:T(8,128)S(1)}, u32[]{:S(2)}, u32[]{:S(2)}) collective-permute-start(f32[2,128,384]{2,1,0:T(8,128)S(1)} %pad_maximum_fusion.12), channel_id=1, source_target_pairs={{1,0},{2,1},{3,2},{4,3},{5,4},{6,5},{7,6},{0,7},{9,8},{10,9},{11,1... | collective-permute-start | bytes 1179656 | tf_op jit(solution)/shard_map/ppermute | solution.py:18
  489.7 71.8 %copy-start.13 = (f32[2,128,128]{2,1,0:T(8,128)S(1)}, f32[2,128,128]{2,1,0:T(8,128)}, u32[]{:S(2)}) copy-start(f32[2,128,128]{2,1,0:T(8,128)} %copy-done.12) | copy-start | bytes 393220
  (9 other events, 10.1 us)
where the time goes:
time: 570 us; the launch traced here: 564 us
  waiting for transfers between devices  167 us (29%)
  local copies, waits for them, and re-layouts  138 us (24%)
  blocking collectives  133 us (23%)
  starting transfers between devices  44.1 us (8%)
  other arithmetic  37.5 us (7%)
  matrix products  20.6 us (4%)
  loops' own time  15.6 us (3%)
  between operations  7.67 us (1%)
    psum x2, blocking collectives, on_device(): lax.psum((numerator, denominator, jnp.sum(alive_flags)), ('scan', 'obj'))  133 us
    ppermute x12, waiting for transfers between devices, with_halo(): lax.ppermute(lax.slice_in_dim(block, block.shape[dim] - width, None, axis...  83.9 us
    ppermute x12, waiting for transfers between devices, with_halo(): lax.ppermute(lax.slice_in_dim(block, 0, width, axis=dim), axis, backward)  83 us
    dynamic_update_slice x4, local copies, waits for them, and re-layouts, deposit(): return lax.dynamic_update_slice(accumulator, existing + slot_piece, corner)  46.5 us
    transpose x4, local copies, waits for them, and re-layouts, transpose_split(): reshaped.transpose(0, 3, 2, 1)  25.7 us
    ppermute x12, starting transfers between devices, with_halo(): lax.ppermute(lax.slice_in_dim(block, block.shape[dim] - width, None, axis...  22.7 us
    ppermute x12, starting transfers between devices, with_halo(): lax.ppermute(lax.slice_in_dim(block, 0, width, axis=dim), axis, backward)  21.4 us
    dot_general x8, matrix products, apply_table(): jnp.dot(flat_rows, dft_table, preferred_element_type=jnp.float32)  20.6 us
  transfers between devices with their start and end apart: 24, of which 22 were waited for; matrix products, arithmetic and copies ran while one was open for 3% of the time, Pallas kernels for 0%

commit v1 on v0

v1 whole, which is shorter than its diff:
```python
import functools

import jax
import jax.numpy as jnp
import numpy as np
from jax import lax
from jax.experimental import pallas as pl
from jax.experimental.pallas import tpu as pltpu
from jax.sharding import PartitionSpec as P

ITERS = 2
MESH = pl.DeviceIdType.MESH
AROUND = [(k, c) for k in (-1, 0, 1) for c in (-1, 0, 1)]


def transform_tables(size):
    indices = np.arange(size, dtype=np.int32)
    phase = (indices[:, None] * indices[None, :] % size).astype(np.float32)
    angles = phase * np.float32(2.0 * 3.141592653589793 / size)
    norm = np.float32(size ** (-0.5))
    cosine, sine = np.cos(angles) * norm, np.sin(angles) * norm
    first = np.block([[cosine, -sine], [sine, cosine]])
    second = np.block([[cosine, sine], [-sine, cosine]])
    return jnp.asarray(np.stack([first, second])).astype(jnp.bfloat16)


def kernel(
    n_scan, n_obj,
    object_ref, probe_ref, patterns_ref, gain_ref, mask_ref, table_ref, centres_ref, live_ref,
    object_out, steps_out, energies_out,
    info, extended, direction_ext, amplitude, power_pad, shifted, coverage, patch, stacked, far, update,
    deposit, fold, fold_x, fold_y, direction, energy_send, energy_recv, sums_x, sums_y,
    info_sem, halo_sem, fold_sem, energy_sem, sums_sem,
):
    tile = object_ref.shape[1]
    size = gain_ref.shape[0]
    modes = probe_ref.shape[0]
    slots = patterns_ref.shape[0]
    extent = tile + size
    my_scan, my_obj = lax.axis_index("scan"), lax.axis_index("obj")

    def at(k, c):
        return {
            "scan": lax.rem(my_scan + (c + n_scan), n_scan),
            "obj": lax.rem(my_obj + (k + n_obj), n_obj),
        }

    def remote(source, target, sems, index, device):
        return pltpu.make_async_remote_copy(
            src_ref=source, dst_ref=target, send_sem=sems.at[(0,) + index],
            recv_sem=sems.at[(1,) + index], device_id=device, device_id_type=MESH,
        )

    partners = [(0, c) for c in range(1, n_scan)] + [(k, 0) for k in range(1, n_obj)]
    partners += [(k, c) for k, c in AROUND if k and c]
    barrier = pltpu.get_barrier_semaphore()
    for k, c in partners:
        pl.semaphore_signal(barrier, inc=1, device_id=at(k, c), device_id_type=MESH)
    pl.semaphore_wait(barrier, len(partners))

    for slot in range(slots):
        info[4, 2 * slot] = centres_ref[slot, 0]
        info[4, 2 * slot + 1] = centres_ref[slot, 1]
    info[4, 2 * slots] = live_ref[0]
    info_copies = [
        remote(info.at[4], info.at[8 - n], info_sem, (n,), at(k, c))
        for n, (k, c) in enumerate(AROUND) if n != 4
    ]

    top, middle, bottom = pl.ds(0, tile), pl.ds(tile, tile), pl.ds(2 * tile, tile)

    def start_gather(source, wide, phase):
        down = remote(source, wide.at[1, :, top, :], halo_sem, (phase, 0), at(1, 0))
        up = remote(source, wide.at[1, :, bottom, :], halo_sem, (phase, 1), at(-1, 0))
        down.start()
        up.start()
        wide[1, :, middle, :] = source[...]

        def sideways(rows, first):
            right = remote(wide.at[1, :, rows, :], wide.at[0, :, rows, :], halo_sem, (phase, first), at(0, 1))
            left = remote(wide.at[1, :, rows, :], wide.at[2, :, rows, :], halo_sem, (phase, first + 1), at(0, -1))
            right.start()
            left.start()
            return [right, left]

        return down, up, sideways, sideways(middle, 2)

    def finish_gather(state):
        down, up, sideways, copies = state
        down.wait_recv()
        copies = copies + sideways(top, 4)
        up.wait_recv()
        copies = copies + sideways(bottom, 6)
        for copy in copies:
            copy.wait()
        down.wait_send()
        up.wait_send()

    state = start_gather(object_ref, extended, 0)
    for copy in info_copies:
        copy.start()

    gain, defect = gain_ref[...], mask_ref[...] == 1
    for slot in range(slots):
        corrected = patterns_ref[slot].astype(jnp.float32) * gain
        mean = 0.25 * (
            pltpu.roll(corrected, 1, 0) + pltpu.roll(corrected, size - 1, 0)
            + pltpu.roll(corrected, 1, 1) + pltpu.roll(corrected, size - 1, 1)
        )
        amplitude[slot] = jnp.sqrt(jnp.where(defect, mean, corrected))
    power = jnp.zeros((size, size), jnp.float32)
    for mode in range(modes):
        power = power + probe_ref[mode, :, :size] ** 2 + probe_ref[mode, :, size:] ** 2
    power_pad[...] = jnp.zeros_like(power_pad)
    for half in range(2):
        power_pad[half, tile : tile + size, :] = power[:, half * tile : (half + 1) * tile]
    for slot in range(slots):
        for column in range(3):
            for plane in range(2):
                zeros = jnp.zeros((tile, tile), jnp.float32)
                deposit[slot, column, plane, :tile, :] = zeros
                deposit[slot, column, plane, tile + size :, :] = zeros
    lane = lax.broadcasted_iota(jnp.int32, (tile, tile), 1)

    for copy in info_copies:
        copy.wait()
    total = jnp.zeros((tile, tile), jnp.float32)
    for n, (k, c) in enumerate(AROUND):
        for slot in range(slots):
            row, column = info[n, 2 * slot], info[n, 2 * slot + 1]
            alive = (slot < info[n, 2 * slots]).astype(jnp.float32)
            rows = pl.ds(2 * tile - tile * k - row, tile)
            low, high = (pltpu.roll(power_pad[half, rows, :], column, 1) for half in range(2))
            if c == 0:
                moved = jnp.where(lane < column, low, high)
            elif c < 0:
                moved = jnp.where(lane < column, high, 0.0)
            else:
                moved = jnp.where(lane < column, 0.0, low)
            shifted[n, slot] = moved
            total = total + moved * alive
    coverage[...] = total
    finish_gather(state)

    wide_lane = lax.broadcasted_iota(jnp.int32, (size, tile), 1)

    def one_slot(slot, carry):
        row, column = centres_ref[slot, 0], centres_ref[slot, 1]
        back_shift = lax.rem(tile - column, tile)
        near = wide_lane < tile - column
        for plane in range(2):
            first, second, third = (
                pltpu.roll(extended[block, plane, pl.ds(row, size), :], back_shift, 1) for block in range(3)
            )
            patch[plane, :, :tile] = jnp.where(near, first, second)
            patch[plane, :, tile:] = jnp.where(near, second, third)
        for mode in range(modes):
            real, imag = patch[0], patch[1]
            probe_real, probe_imag = probe_ref[mode, :, :size], probe_ref[mode, :, size:]
            exit_wave = jnp.concatenate(
                [real * probe_real - imag * probe_imag, real * probe_imag + imag * probe_real], axis=1
            ).astype(jnp.bfloat16)
            half = jnp.dot(exit_wave, table_ref[0], preferred_element_type=jnp.float32).astype(jnp.bfloat16)
            stacked[mode, :size, :] = half[:, :size]
            stacked[mode, size:, :] = half[:, size:]
            far[mode] = jnp.dot(table_ref[1], stacked[mode], preferred_element_type=jnp.float32)
        model = jnp.zeros((size, size), jnp.float32)
        for mode in range(modes):
            model = model + far[mode, :size, :] ** 2 + far[mode, size:, :] ** 2
        ratio = amplitude[slot] * lax.rsqrt(jnp.maximum(model, 0.25))
        power = jnp.concatenate([power_pad[half, tile : tile + size, :] for half in range(2)], axis=1)
        update[0] = -power * patch[0]
        update[1] = -power * patch[1]
        for mode in range(modes):
            stacked[mode, :size, :] = (far[mode, :size, :] * ratio).astype(jnp.bfloat16)
            stacked[mode, size:, :] = (far[mode, size:, :] * ratio).astype(jnp.bfloat16)
            back = jnp.dot(table_ref[0], stacked[mode], preferred_element_type=jnp.float32).astype(jnp.bfloat16)
            back = jnp.concatenate([back[:size], back[size:]], axis=1)
            wave = jnp.dot(back, table_ref[1], preferred_element_type=jnp.float32)
            real, imag = wave[:, :size], wave[:, size:]
            probe_real, probe_imag = probe_ref[mode, :, :size], probe_ref[mode, :, size:]
            update[0] += real * probe_real + imag * probe_imag
            update[1] += imag * probe_real - real * probe_imag
        alive = (slot < live_ref[0]).astype(jnp.float32)
        far_lane = wide_lane < column
        for plane in range(2):
            low = pltpu.roll(update[plane, :, :tile] * alive, column, 1)
            high = pltpu.roll(update[plane, :, tile:] * alive, column, 1)
            deposit[slot, 0, plane, tile : tile + size, :] = jnp.where(far_lane, 0.0, low)
            deposit[slot, 1, plane, tile : tile + size, :] = jnp.where(far_lane, low, high)
            deposit[slot, 2, plane, tile : tile + size, :] = jnp.where(far_lane, high, 0.0)
        return carry

    row_id = lax.broadcasted_iota(jnp.int32, (8, tile), 0)

    def as_row(value, row):
        return jnp.where(row_id == row, jnp.sum(value, axis=0, keepdims=True), 0.0)

    steps, energies = [], []
    live_number = (live_ref[0]).astype(jnp.float32)
    for iteration in range(ITERS):
        lax.fori_loop(0, slots, one_slot, 0)

        for column in (0, 2, 1):
            for plane in range(2):
                summed = deposit[0, column, plane, pl.ds(tile - centres_ref[0, 0], extent), :]
                for slot in range(1, slots):
                    summed = summed + deposit[slot, column, plane, pl.ds(tile - centres_ref[slot, 0], extent), :]
                fold[iteration, column, plane] = summed
        sides = []
        for place, rows in enumerate((top, bottom, middle)):
            right = remote(
                fold.at[iteration, 2, :, rows, :], fold_x.at[iteration, 0, :, rows, :],
                fold_sem, (iteration, 2 * place), at(0, 1),
            )
            left = remote(
                fold.at[iteration, 0, :, rows, :], fold_x.at[iteration, 1, :, rows, :],
                fold_sem, (iteration, 2 * place + 1), at(0, -1),
            )
            right.start()
            left.start()
            sides.append((rows, right, left))

        def add_sides(side):
            rows, right, left = side
            right.wait_recv()
            left.wait_recv()
            fold[iteration, 1, :, rows, :] = (
                fold[iteration, 1, :, rows, :] + fold_x[iteration, 0, :, rows, :] + fold_x[iteration, 1, :, rows, :]
            )

        add_sides(sides[0])
        up = remote(fold.at[iteration, 1, :, top, :], fold_y.at[iteration, 0], fold_sem, (iteration, 6), at(-1, 0))
        up.start()
        add_sides(sides[1])
        down = remote(fold.at[iteration, 1, :, bottom, :], fold_y.at[iteration, 1], fold_sem, (iteration, 7), at(1, 0))
        down.start()
        add_sides(sides[2])
        up.wait_recv()
        down.wait_recv()
        gradient = fold[iteration, 1, :, middle, :] + fold_y[iteration, 0] + fold_y[iteration, 1]
        cover = coverage[...]
        moved = gradient / (cover + 0.5)[None]
        direction[iteration] = moved
        last = iteration == ITERS - 1
        if not last:
            state = start_gather(direction.at[iteration], direction_ext, 1 + iteration)

        squares = moved[0] * moved[0] + moved[1] * moved[1]
        sums_x[iteration, my_scan] = (
            as_row(moved[0] * gradient[0] + moved[1] * gradient[1], 0)
            + as_row(cover * squares, 1) + jnp.where(row_id == 2, live_number, 0.0)
        )
        sums = []
        for other in range(1, n_scan):
            mine = sums_x.at[iteration, my_scan]
            sums.append(remote(mine, mine, sums_sem, (iteration, other), at(0, other)))
            sums[-1].start()
        energy_copies = []
        for n, (k, c) in enumerate(AROUND):
            block = jnp.zeros((8, tile), jnp.float32)
            for slot in range(slots):
                block = block + as_row(squares * shifted[n, slot], slot)
            if n == 4:
                energy_recv[iteration, n] = block
            else:
                energy_send[iteration, n] = block
                copy = remote(
                    energy_send.at[iteration, n], energy_recv.at[iteration, n],
                    energy_sem, (iteration, n), at(k, c),
                )
                copy.start()
                energy_copies.append(copy)
        for copy in sums:
            copy.wait()
        sums_y[iteration, my_obj] = jnp.sum(sums_x[iteration], axis=0)
        sums = []
        for other in range(1, n_obj):
            mine = sums_y.at[iteration, my_obj]
            sums.append(remote(mine, mine, sums_sem, (iteration, n_scan + other), at(other, 0)))
            sums[-1].start()
        for copy in energy_copies:
            copy.wait()
        energy = jnp.sum(energy_recv[iteration], axis=0)
        energy = jnp.sum(energy, axis=1, keepdims=True)
        for copy in sums:
            copy.wait()
        everywhere = jnp.sum(sums_y[iteration], axis=0)
        rows = jnp.sum(everywhere, axis=1, keepdims=True)
        step = rows[0:1] / rows[1:2]
        steps.append(step)
        live_total = rows[2:3] * (1.0 / tile)
        energies.append(energy * (live_total / rows[1:2]))
        for rows, right, left in sides:
            right.wait_send()
            left.wait_send()
        up.wait_send()
        down.wait_send()
        if not last:
            finish_gather(state)
            extended[...] = extended[...] + step.reshape(1, 1, 1, 1) * direction_ext[...]
        else:
            object_out[...] = extended[1, :, middle, :] + step.reshape(1, 1, 1) * direction[iteration]
    for iteration in range(ITERS):
        steps_out[iteration] = steps[iteration][0, 0]
        for slot in range(slots):
            alive = (slot < live_ref[0]).astype(jnp.float32)
            energies_out[iteration, slot] = energies[iteration][slot, 0] * alive


def on_device(n_scan, n_obj, object_field, probe_modes, patterns, gain_map, defect_mask, probe_centres, live_counts):
    tile = object_field.shape[1]
    modes, size = probe_modes.shape[0], probe_modes.shape[1]
    slots = patterns.shape[0]
    extent = tile + size
    table = transform_tables(size)
    f32 = jnp.float32
    vmem, smem = pl.BlockSpec(memory_space=pltpu.VMEM), pl.BlockSpec(memory_space=pltpu.SMEM)
    flops = ITERS * slots * modes * 4 * 2 * size * (2 * size) ** 2
    outputs = pl.pallas_call(
        functools.partial(kernel, n_scan, n_obj),
        out_shape=(
            jax.ShapeDtypeStruct(object_field.shape, f32),
            jax.ShapeDtypeStruct((ITERS,), f32),
            jax.ShapeDtypeStruct((ITERS, slots), f32),
        ),
        in_specs=[vmem] * 6 + [smem] * 2,
        out_specs=(vmem, smem, smem),
        scratch_shapes=[
            pltpu.SMEM((9, 128), jnp.int32),
            pltpu.VMEM((3, 2, extent, tile), f32),
            pltpu.VMEM((3, 2, extent, tile), f32),
            pltpu.VMEM((slots, size, size), f32),
            pltpu.VMEM((2, size + 2 * tile, tile), f32),
            pltpu.VMEM((9, slots, tile, tile), f32),
            pltpu.VMEM((tile, tile), f32),
            pltpu.VMEM((2, size, size), f32),
            pltpu.VMEM((modes, 2 * size, size), jnp.bfloat16),
            pltpu.VMEM((modes, 2 * size, size), f32),
            pltpu.VMEM((2, size, size), f32),
            pltpu.VMEM((slots, 3, 2, size + 2 * tile, tile), f32),
            pltpu.VMEM((ITERS, 3, 2, extent, tile), f32),
            pltpu.VMEM((ITERS, 2, 2, extent, tile), f32),
            pltpu.VMEM((ITERS, 2, 2, tile, tile), f32),
            pltpu.VMEM((ITERS, 2, tile, tile), f32),
            pltpu.VMEM((ITERS, 9, 8, tile), f32),
            pltpu.VMEM((ITERS, 9, 8, tile), f32),
            pltpu.VMEM((ITERS, n_scan, 8, tile), f32),
            pltpu.VMEM((ITERS, n_obj, 8, tile), f32),
            pltpu.SemaphoreType.DMA((2, 9)),
            pltpu.SemaphoreType.DMA((2, ITERS, 8)),
            pltpu.SemaphoreType.DMA((2, ITERS, 8)),
            pltpu.SemaphoreType.DMA((2, ITERS, 9)),
            pltpu.SemaphoreType.DMA((2, ITERS, n_scan + n_obj)),
        ],
        compiler_params=pltpu.CompilerParams(
            collective_id=0, has_side_effects=True, vmem_limit_bytes=48 * 1024 * 1024
        ),
        cost_estimate=pl.CostEstimate(flops=flops, bytes_accessed=8 * 1024 * 1024, transcendentals=0),
    )(object_field, probe_modes, patterns, gain_map, defect_mask, table, probe_centres, live_counts)
    return tuple(outputs)


def solution(mesh):
    placed = (
        P(None, "obj", "scan"),
        P(),
        P(("scan", "obj"), None, None),
        P(),
        P(),
        P(("scan", "obj"), None),
        P(("scan", "obj")),
    )
    return jax.shard_map(
        functools.partial(on_device, mesh.shape["scan"], mesh.shape["obj"]),
        mesh=mesh,
        in_specs=placed,
        out_specs=(P(None, "obj", "scan"), P(), P(None, ("scan", "obj"))),
        check_vma=False,
    )
```

time: 570 us -> 112 us (0.20); the launches traced: 564 us -> 111 us
  waiting for transfers between devices: 167 us -> 0 us
  blocking collectives: 133 us -> 0 us
  local copies, waits for them, and re-layouts: 138 us -> 8.97 us
  Pallas kernels: 0 us -> 101 us
  starting transfers between devices: 44.1 us -> 0 us
  other arithmetic: 37.5 us -> 0 us
  matrix products: 20.6 us -> 0 us
  loops' own time: 15.6 us -> 0 us
  between operations: 7.67 us -> 1.3 us
    ppermute x24 -> x0, waiting for transfers between devices: 167 us -> none  [the longest x12 83.9 us: with_halo(): lax.ppermute(lax.slice_in_dim(block, block.shape[dim] - width, None, axis...]
    psum x2 -> x0, blocking collectives: 133 us -> none  [on_device(): lax.psum((numerator, denominator, jnp.sum(alive_flags)), ('scan', 'obj'))]
    pallas_call x0 -> x1, Pallas kernels: none -> 101 us  [on_device(): pl.pallas_call(functools.partial(kernel, n_scan, n_obj), out_shape=(jax.S...]
    dynamic_update_slice x4 -> x0, local copies, waits for them, and re-layouts: 46.5 us -> none  [deposit(): return lax.dynamic_update_slice(accumulator, existing + slot_piece, corner)]
    ppermute x24 -> x0, starting transfers between devices: 44.1 us -> none  [the longest x12 22.7 us: with_halo(): lax.ppermute(lax.slice_in_dim(block, block.shape[dim] - width, None, axis...]
    transpose x4 -> x0, local copies, waits for them, and re-layouts: 25.7 us -> none  [transpose_split(): reshaped.transpose(0, 3, 2, 1)]
    dot_general x8 -> x0, matrix products: 20.6 us -> none  [apply_table(): jnp.dot(flat_rows, dft_table, preferred_element_type=jnp.float32)]
    gather x24 -> x0, local copies, waits for them, and re-layouts: 18.8 us -> none
  transfers between devices with their start and end apart: 24 -> 0, of which waited for: 22 -> 0; matrix products, arithmetic and copies ran while one was open for 3% -> 0% of each run, Pallas kernels for 0% -> 0%
where the time goes in v1:
time: 112 us; the launch traced here: 111 us
  Pallas kernels  101 us (90%)
  local copies, waits for them, and re-layouts  8.97 us (8%)
  between operations  1.3 us (1%)
    pallas_call x1, Pallas kernels, on_device(): pl.pallas_call(functools.partial(kernel, n_scan, n_obj), out_shape=(jax.S...  101 us
    unnamed x17, local copies, waits for them, and re-layouts  8.97 us

profile of v1, /device:TPU:1, one launch (start us, length us, event | category | flops | bytes accessed | tf_op | source)
XLA Modules:
  0.0 111.4 jit_solution(9127701666923006558)
XLA Ops:
  1.3 0.0 copy-start
  1.3 1.6 %copy-done = f32[4,256,512]{2,1,0:T(8,128)S(1)} copy-done((f32[4,256,512]{2,1,0:T(8,128)S(1)}, f32[4,256,512]{2,1,0:T(8,128)}, u32[]{:S(2)}) %copy-start) | copy-done | bytes 2097176
  2.9 0.0 copy-start.1
  2.9 0.9 copy-done.1
  3.8 0.0 copy-start.2
  3.8 0.9 copy-done.2
  4.8 0.0 copy-start.3
  4.8 0.9 copy-done.3
  5.7 0.0 copy-start.4
  5.7 0.9 copy-done.4
  6.6 0.0 copy-start.5
  6.6 0.7 copy-done.5
  7.3 0.0 copy-start.6
  7.3 1.2 %copy-done.6 = bf16[2,512,512]{2,1,0:T(8,128)(2,1)S(1)} copy-done((bf16[2,512,512]{2,1,0:T(8,128)(2,1)S(1)}, bf16[2,512,512]{2,1,0:T(8,128)(2,1)}, u32[]{:S(2)}) %copy-start.6) | copy-done | bytes 1048600
  8.5 101.1 %shard_map.103 = (f32[2,128,128]{2,1,0:T(8,128)S(1)}, f32[2]{0:T(128)S(1)}, f32[2,2]{1,0:T(2,128)S(1)}) custom-call(f32[2,128,128]{2,1,0:T(8,128)S(1)} %copy-done.4, f32[4,256,512]{2,1,0:T(8,128)S(1)} %copy-done, bf16[2,256,256]{2,1,0:T(8,128)(2,1)S(1)} %copy-done.1, f32[256,256]{1,0:T(8,128)S(1)} %copy-done.2, s32[256,256]{1,0:T(8,128)S(1)} %copy-done.3, ...), custom_call_target="tpu_custom_call" | custom-call | flops 8589934592 | bytes 8388608 | tf_op jit(solution)/shard_map/pallas_call | solution.py:320
  109.7 0.7 copy.15
  110.3 0.5 copy.16
  110.8 0.6 copy.17
Async XLA Ops:
  1.3 1.6 %copy-start = (f32[4,256,512]{2,1,0:T(8,128)S(1)}, f32[4,256,512]{2,1,0:T(8,128)}, u32[]{:S(2)}) copy-start(f32[4,256,512]{2,1,0:T(8,128)} %probe_ref.1) | copy-start | bytes 6291460
  2.9 0.9 copy-start.1
  3.8 0.9 copy-start.2
  4.8 0.9 copy-start.3
  5.7 0.9 copy-start.4
  6.6 0.7 copy-start.5
  7.3 1.2 %copy-start.6 = (bf16[2,512,512]{2,1,0:T(8,128)(2,1)S(1)}, bf16[2,512,512]{2,1,0:T(8,128)(2,1)}, u32[]{:S(2)}) copy-start(bf16[2,512,512]{2,1,0:T(8,128)(2,1)} %constant.6.table_ref) | copy-start | bytes 3145732

commit v2 on v1

--- a/solution.py
+++ b/solution.py
@@ -26,18 +26,19 @@
 
 def kernel(
     n_scan, n_obj,
-    object_ref, probe_ref, patterns_ref, gain_ref, mask_ref, table_ref, centres_ref, live_ref,
+    object_hbm, probe_hbm, patterns_hbm, gain_hbm, mask_hbm, table_hbm, centres_hbm, live_hbm,
     object_out, steps_out, energies_out,
+    probe_ref, patterns_ref, gain_ref, mask_ref, table_ref, centres_ref, live_ref,
     info, extended, direction_ext, amplitude, power_pad, shifted, coverage, patch, stacked, far, update,
-    deposit, fold, fold_x, fold_y, direction, energy_send, energy_recv, sums_x, sums_y,
-    info_sem, halo_sem, fold_sem, energy_sem, sums_sem,
+    deposit, fold, fold_x, fold_y, energy_send, energy_recv, sums_x, sums_y,
+    load_sem, info_sem, halo_sem, fold_sem, energy_sem, sums_sem,
 ):
-    tile = object_ref.shape[1]
+    tile = object_hbm.shape[1]
     size = gain_ref.shape[0]
     modes = probe_ref.shape[0]
     slots = patterns_ref.shape[0]
-    extent = tile + size
     my_scan, my_obj = lax.axis_index("scan"), lax.axis_index("obj")
+    top, middle, bottom = pl.ds(0, tile), pl.ds(tile, tile), pl.ds(2 * tile, tile)
 
     def at(k, c):
         return {
@@ -50,6 +51,17 @@
             src_ref=source, dst_ref=target, send_sem=sems.at[(0,) + index],
             recv_sem=sems.at[(1,) + index], device_id=device, device_id_type=MESH,
         )
+
+    pairs = (
+        (object_hbm, extended.at[1, :, middle, :]), (centres_hbm, centres_ref), (live_hbm, live_ref),
+        (patterns_hbm, patterns_ref), (gain_hbm, gain_ref), (mask_hbm, mask_ref),
+        (probe_hbm, probe_ref), (table_hbm, table_ref),
+    )
+    loads = [
+        pltpu.make_async_copy(source, target, load_sem.at[n]) for n, (source, target) in enumerate(pairs)
+    ]
+    for load in loads:
+        load.start()
 
     partners = [(0, c) for c in range(1, n_scan)] + [(k, 0) for k in range(1, n_obj)]
     partners += [(k, c) for k, c in AROUND if k and c]
@@ -58,6 +70,45 @@
         pl.semaphore_signal(barrier, inc=1, device_id=at(k, c), device_id_type=MESH)
     pl.semaphore_wait(barrier, len(partners))
 
+    def start_gather(wide, phase):
+        along = []
+        for plane in range(2):
+            mine = wide.at[1, plane, middle, :]
+            along.append(remote(mine, wide.at[1, plane, top, :], halo_sem, (phase, 2 * plane), at(1, 0)))
+            along.append(remote(mine, wide.at[1, plane, bottom, :], halo_sem, (phase, 2 * plane + 1), at(-1, 0)))
+        for copy in along:
+            copy.start()
+        return along, [send_sideways(wide, phase, plane, middle, 4 + 2 * plane) for plane in range(2)]
+
+    def send_sideways(wide, phase, plane, rows, first):
+        mine = wide.at[1, plane, rows, :]
+        pair = (
+            remote(mine, wide.at[0, plane, rows, :], halo_sem, (phase, first), at(0, 1)),
+            remote(mine, wide.at[2, plane, rows, :], halo_sem, (phase, first + 1), at(0, -1)),
+        )
+        for copy in pair:
+            copy.start()
+        return pair
+
+    def pass_on(wide, phase, along, beside):
+        beside = list(beside)
+        for n, copy in enumerate(along):
+            copy.wait_recv()
+            beside.append(send_sideways(wide, phase, n // 2, bottom if n % 2 else top, 8 + 2 * n))
+        return beside
+
+    def finish_gather(along, beside):
+        for pair in beside:
+            for copy in pair:
+                copy.wait()
+        for copy in along:
+            copy.wait_send()
+
+    loads[0].wait()
+    along, beside = start_gather(extended, 0)
+
+    loads[1].wait()
+    loads[2].wait()
     for slot in range(slots):
         info[4, 2 * slot] = centres_ref[slot, 0]
         info[4, 2 * slot + 1] = centres_ref[slot, 1]
@@ -66,40 +117,11 @@
         remote(info.at[4], info.at[8 - n], info_sem, (n,), at(k, c))
         for n, (k, c) in enumerate(AROUND) if n != 4
     ]
-
-    top, middle, bottom = pl.ds(0, tile), pl.ds(tile, tile), pl.ds(2 * tile, tile)
-
-    def start_gather(source, wide, phase):
-        down = remote(source, wide.at[1, :, top, :], halo_sem, (phase, 0), at(1, 0))
-        up = remote(source, wide.at[1, :, bottom, :], halo_sem, (phase, 1), at(-1, 0))
-        down.start()
-        up.start()
-        wide[1, :, middle, :] = source[...]
-
-        def sideways(rows, first):
-            right = remote(wide.at[1, :, rows, :], wide.at[0, :, rows, :], halo_sem, (phase, first), at(0, 1))
-            left = remote(wide.at[1, :, rows, :], wide.at[2, :, rows, :], halo_sem, (phase, first + 1), at(0, -1))
-            right.start()
-            left.start()
-            return [right, left]
-
-        return down, up, sideways, sideways(middle, 2)
-
-    def finish_gather(state):
-        down, up, sideways, copies = state
-        down.wait_recv()
-        copies = copies + sideways(top, 4)
-        up.wait_recv()
-        copies = copies + sideways(bottom, 6)
-        for copy in copies:
-            copy.wait()
-        down.wait_send()
-        up.wait_send()
-
-    state = start_gather(object_ref, extended, 0)
     for copy in info_copies:
         copy.start()
 
+    for load in loads[3:6]:
+        load.wait()
     gain, defect = gain_ref[...], mask_ref[...] == 1
     for slot in range(slots):
         corrected = patterns_ref[slot].astype(jnp.float32) * gain
@@ -108,6 +130,7 @@
             + pltpu.roll(corrected, 1, 1) + pltpu.roll(corrected, size - 1, 1)
         )
         amplitude[slot] = jnp.sqrt(jnp.where(defect, mean, corrected))
+    loads[6].wait()
     power = jnp.zeros((size, size), jnp.float32)
     for mode in range(modes):
         power = power + probe_ref[mode, :, :size] ** 2 + probe_ref[mode, :, size:] ** 2
@@ -120,10 +143,12 @@
                 zeros = jnp.zeros((tile, tile), jnp.float32)
                 deposit[slot, column, plane, :tile, :] = zeros
                 deposit[slot, column, plane, tile + size :, :] = zeros
-    lane = lax.broadcasted_iota(jnp.int32, (tile, tile), 1)
+    beside = pass_on(extended, 0, along, beside)
+    loads[7].wait()
 
     for copy in info_copies:
         copy.wait()
+    lane = lax.broadcasted_iota(jnp.int32, (tile, tile), 1)
     total = jnp.zeros((tile, tile), jnp.float32)
     for n, (k, c) in enumerate(AROUND):
         for slot in range(slots):
@@ -140,7 +165,7 @@
             shifted[n, slot] = moved
             total = total + moved * alive
     coverage[...] = total
-    finish_gather(state)
+    finish_gather(along, beside)
 
     wide_lane = lax.broadcasted_iota(jnp.int32, (size, tile), 1)
 
@@ -196,67 +221,85 @@
     def as_row(value, row):
         return jnp.where(row_id == row, jnp.sum(value, axis=0, keepdims=True), 0.0)
 
-    steps, energies = [], []
-    live_number = (live_ref[0]).astype(jnp.float32)
+    live_number = live_ref[0].astype(jnp.float32)
+
+    def sum_start(table, mine, base, count, where, iteration):
+        copies = []
+        for other in range(1, count):
+            block = table.at[iteration, mine]
+            copies.append(remote(block, block, sums_sem, (iteration, base + other), where(other)))
+            copies[-1].start()
+        return copies
+
+    energy_copies, scales = [], []
     for iteration in range(ITERS):
         lax.fori_loop(0, slots, one_slot, 0)
 
-        for column in (0, 2, 1):
-            for plane in range(2):
-                summed = deposit[0, column, plane, pl.ds(tile - centres_ref[0, 0], extent), :]
-                for slot in range(1, slots):
-                    summed = summed + deposit[slot, column, plane, pl.ds(tile - centres_ref[slot, 0], extent), :]
-                fold[iteration, column, plane] = summed
-        sides = []
-        for place, rows in enumerate((top, bottom, middle)):
-            right = remote(
-                fold.at[iteration, 2, :, rows, :], fold_x.at[iteration, 0, :, rows, :],
-                fold_sem, (iteration, 2 * place), at(0, 1),
+        def gathered(column, plane, block):
+            summed = None
+            for slot in range(slots):
+                rows = pl.ds((block + 1) * tile - centres_ref[slot, 0], tile)
+                term = deposit[slot, column, plane, rows, :]
+                summed = term if summed is None else summed + term
+            return summed
+
+        sides = {}
+        blocks = (top, middle, bottom)
+        for place, (plane, block) in enumerate(((0, 0), (0, 2), (1, 0), (1, 2), (0, 1), (1, 1))):
+            rows = blocks[block]
+            pair = []
+            for side, (column, step) in enumerate(((2, 1), (0, -1))):
+                fold[iteration, column, plane, rows, :] = gathered(column, plane, block)
+                copy = remote(
+                    fold.at[iteration, column, plane, rows, :], fold_x.at[iteration, side, plane, rows, :],
+                    fold_sem, (iteration, 2 * place + side), at(0, step),
+                )
+                copy.start()
+                pair.append(copy)
+            sides[plane, block] = pair
+        for plane in range(2):
+            for block in (0, 2, 1):
+                fold[iteration, 1, plane, blocks[block], :] = gathered(1, plane, block)
+
+        def add_sides(plane, block):
+            rows = blocks[block]
+            for copy in sides[plane, block]:
+                copy.wait_recv()
+            return (
+                fold[iteration, 1, plane, rows, :]
+                + fold_x[iteration, 0, plane, rows, :] + fold_x[iteration, 1, plane, rows, :]
             )
-            left = remote(
-                fold.at[iteration, 0, :, rows, :], fold_x.at[iteration, 1, :, rows, :],
-                fold_sem, (iteration, 2 * place + 1), at(0, -1),
-            )
-            right.start()
-            left.start()
-            sides.append((rows, right, left))
-
-        def add_sides(side):
-            rows, right, left = side
-            right.wait_recv()
-            left.wait_recv()
-            fold[iteration, 1, :, rows, :] = (
-                fold[iteration, 1, :, rows, :] + fold_x[iteration, 0, :, rows, :] + fold_x[iteration, 1, :, rows, :]
-            )
-
-        add_sides(sides[0])
-        up = remote(fold.at[iteration, 1, :, top, :], fold_y.at[iteration, 0], fold_sem, (iteration, 6), at(-1, 0))
-        up.start()
-        add_sides(sides[1])
-        down = remote(fold.at[iteration, 1, :, bottom, :], fold_y.at[iteration, 1], fold_sem, (iteration, 7), at(1, 0))
-        down.start()
-        add_sides(sides[2])
-        up.wait_recv()
-        down.wait_recv()
-        gradient = fold[iteration, 1, :, middle, :] + fold_y[iteration, 0] + fold_y[iteration, 1]
+
+        folds = []
+        for plane in range(2):
+            for side, (block, step) in enumerate(((0, -1), (2, 1))):
+                rows = blocks[block]
+                fold[iteration, 1, plane, rows, :] = add_sides(plane, block)
+                copy = remote(
+                    fold.at[iteration, 1, plane, rows, :], fold_y.at[iteration, side, plane],
+                    fold_sem, (iteration, 12 + 2 * plane + side), at(step, 0),
+                )
+                copy.start()
+                folds.append(copy)
+        own = [add_sides(plane, 1) for plane in range(2)]
         cover = coverage[...]
-        moved = gradient / (cover + 0.5)[None]
-        direction[iteration] = moved
+        gradient, moved = [], []
+        for plane in range(2):
+            folds[2 * plane].wait_recv()
+            folds[2 * plane + 1].wait_recv()
+            gradient.append(own[plane] + fold_y[iteration, 0, plane] + fold_y[iteration, 1, plane])
+            moved.append(gradient[plane] / (cover + 0.5))
+            direction_ext[iteration, 1, plane, middle, :] = moved[plane]
         last = iteration == ITERS - 1
         if not last:
-            state = start_gather(direction.at[iteration], direction_ext, 1 + iteration)
+            along, beside = start_gather(direction_ext.at[iteration], 1 + iteration)
 
         squares = moved[0] * moved[0] + moved[1] * moved[1]
         sums_x[iteration, my_scan] = (
             as_row(moved[0] * gradient[0] + moved[1] * gradient[1], 0)
             + as_row(cover * squares, 1) + jnp.where(row_id == 2, live_number, 0.0)
         )
-        sums = []
-        for other in range(1, n_scan):
-            mine = sums_x.at[iteration, my_scan]
-            sums.append(remote(mine, mine, sums_sem, (iteration, other), at(0, other)))
-            sums[-1].start()
-        energy_copies = []
+        first_sums = sum_start(sums_x, my_scan, 0, n_scan, lambda other: at(0, other), iteration)
         for n, (k, c) in enumerate(AROUND):
             block = jnp.zeros((8, tile), jnp.float32)
             for slot in range(slots):
@@ -271,41 +314,39 @@
                 )
                 copy.start()
                 energy_copies.append(copy)
-        for copy in sums:
+        for copy in first_sums:
             copy.wait()
         sums_y[iteration, my_obj] = jnp.sum(sums_x[iteration], axis=0)
-        sums = []
-        for other in range(1, n_obj):
-            mine = sums_y.at[iteration, my_obj]
-            sums.append(remote(mine, mine, sums_sem, (iteration, n_scan + other), at(other, 0)))
-            sums[-1].start()
-        for copy in energy_copies:
-            copy.wait()
-        energy = jnp.sum(energy_recv[iteration], axis=0)
-        energy = jnp.sum(energy, axis=1, keepdims=True)
-        for copy in sums:
+        second_sums = sum_start(sums_y, my_obj, n_scan, n_obj, lambda other: at(other, 0), iteration)
+        if not last:
+            beside = pass_on(direction_ext.at[iteration], 1 + iteration, along, beside)
+        for pair in sides.values():
+            for copy in pair:
+                copy.wait_send()
+        for copy in folds:
+            copy.wait_send()
+        for copy in second_sums:
             copy.wait()
         everywhere = jnp.sum(sums_y[iteration], axis=0)
         rows = jnp.sum(everywhere, axis=1, keepdims=True)
         step = rows[0:1] / rows[1:2]
-        steps.append(step)
-        live_total = rows[2:3] * (1.0 / tile)
-        energies.append(energy * (live_total / rows[1:2]))
-        for rows, right, left in sides:
-            right.wait_send()
-            left.wait_send()
-        up.wait_send()
-        down.wait_send()
+        scales.append((step, rows[2:3] * (1.0 / tile) / rows[1:2]))
         if not last:
-            finish_gather(state)
-            extended[...] = extended[...] + step.reshape(1, 1, 1, 1) * direction_ext[...]
+            finish_gather(along, beside)
+            extended[...] = extended[...] + step.reshape(1, 1, 1, 1) * direction_ext[iteration]
         else:
-            object_out[...] = extended[1, :, middle, :] + step.reshape(1, 1, 1) * direction[iteration]
+            object_out[...] = (
+                extended[1, :, middle, :] + step.reshape(1, 1, 1) * direction_ext[iteration, 1, :, middle, :]
+            )
+    for copy in energy_copies:
+        copy.wait()
     for iteration in range(ITERS):
-        steps_out[iteration] = steps[iteration][0, 0]
+        step, scale = scales[iteration]
+        steps_out[iteration] = step[0, 0]
+        energy = jnp.sum(jnp.sum(energy_recv[iteration], axis=0), axis=1, keepdims=True) * scale
         for slot in range(slots):
             alive = (slot < live_ref[0]).astype(jnp.float32)
-            energies_out[iteration, slot] = energies[iteration][slot, 0] * alive
+            energies_out[iteration, slot] = energy[slot, 0] * alive
 
 
 def on_device(n_scan, n_obj, object_field, probe_modes, patterns, gain_map, defect_mask, probe_centres, live_counts):
@@ -316,6 +357,7 @@
     table = transform_tables(size)
     f32 = jnp.float32
     vmem, smem = pl.BlockSpec(memory_space=pltpu.VMEM), pl.BlockSpec(memory_space=pltpu.SMEM)
+    hbm = pl.BlockSpec(memory_space=pltpu.HBM)
     flops = ITERS * slots * modes * 4 * 2 * size * (2 * size) ** 2
     outputs = pl.pallas_call(
         functools.partial(kernel, n_scan, n_obj),
@@ -324,12 +366,19 @@
             jax.ShapeDtypeStruct((ITERS,), f32),
             jax.ShapeDtypeStruct((ITERS, slots), f32),
         ),
-        in_specs=[vmem] * 6 + [smem] * 2,
+        in_specs=[hbm] * 8,
         out_specs=(vmem, smem, smem),
         scratch_shapes=[
+            pltpu.VMEM(probe_modes.shape, f32),
+            pltpu.VMEM(patterns.shape, patterns.dtype),
+            pltpu.VMEM(gain_map.shape, f32),
+            pltpu.VMEM(defect_mask.shape, jnp.int32),
+            pltpu.VMEM(table.shape, table.dtype),
+            pltpu.SMEM(probe_centres.shape, jnp.int32),
+            pltpu.SMEM(live_counts.shape, jnp.int32),
             pltpu.SMEM((9, 128), jnp.int32),
             pltpu.VMEM((3, 2, extent, tile), f32),
-            pltpu.VMEM((3, 2, extent, tile), f32),
+            pltpu.VMEM((ITERS, 3, 2, extent, tile), f32),
             pltpu.VMEM((slots, size, size), f32),
             pltpu.VMEM((2, size + 2 * tile, tile), f32),
             pltpu.VMEM((9, slots, tile, tile), f32),
@@ -342,19 +391,19 @@
             pltpu.VMEM((ITERS, 3, 2, extent, tile), f32),
             pltpu.VMEM((ITERS, 2, 2, extent, tile), f32),
             pltpu.VMEM((ITERS, 2, 2, tile, tile), f32),
-            pltpu.VMEM((ITERS, 2, tile, tile), f32),
             pltpu.VMEM((ITERS, 9, 8, tile), f32),
             pltpu.VMEM((ITERS, 9, 8, tile), f32),
             pltpu.VMEM((ITERS, n_scan, 8, tile), f32),
             pltpu.VMEM((ITERS, n_obj, 8, tile), f32),
+            pltpu.SemaphoreType.DMA((8,)),
             pltpu.SemaphoreType.DMA((2, 9)),
-            pltpu.SemaphoreType.DMA((2, ITERS, 8)),
-            pltpu.SemaphoreType.DMA((2, ITERS, 8)),
+            pltpu.SemaphoreType.DMA((2, ITERS, 16)),
+            pltpu.SemaphoreType.DMA((2, ITERS, 16)),
             pltpu.SemaphoreType.DMA((2, ITERS, 9)),
             pltpu.SemaphoreType.DMA((2, ITERS, n_scan + n_obj)),
         ],
         compiler_params=pltpu.CompilerParams(
-            collective_id=0, has_side_effects=True, vmem_limit_bytes=48 * 1024 * 1024
+            collective_id=0, has_side_effects=True, vmem_limit_bytes=62 * 1024 * 1024
         ),
         cost_estimate=pl.CostEstimate(flops=flops, bytes_accessed=8 * 1024 * 1024, transcendentals=0),
     )(object_field, probe_modes, patterns, gain_map, defect_mask, table, probe_centres, live_counts)

time: 112 us -> 99.2 us (0.89)
  Pallas kernels: 101 us -> 93.8 us
  local copies, waits for them, and re-layouts: 8.97 us -> 3.96 us
    pallas_call x1, Pallas kernels: 101 us -> 93.8 us  [on_device(): pl.pallas_call(functools.partial(kernel, n_scan, n_obj), out_shape=(jax.S...]
    unnamed x17 -> x3, local copies, waits for them, and re-layouts: 8.97 us -> 3.96 us
where the time goes in v2:
time: 99.2 us; the launch traced here: 99.1 us
  Pallas kernels  93.8 us (95%)
  local copies, waits for them, and re-layouts  3.96 us (4%)
  between operations  1.29 us (1%)
    pallas_call x1, Pallas kernels, on_device(): pl.pallas_call(functools.partial(kernel, n_scan, n_obj), out_shape=(jax.S...  93.8 us
    unnamed x3, local copies, waits for them, and re-layouts  3.96 us

profile of v2, /device:TPU:1, one launch (start us, length us, event | category | flops | bytes accessed | tf_op | source)
XLA Modules:
  0.0 99.1 jit_solution(3817263524241193730)
XLA Ops:
  1.3 93.8 %shard_map.103 = (f32[2,128,128]{2,1,0:T(8,128)}, f32[2]{0:T(128)}, f32[2,2]{1,0:T(2,128)}) custom-call(f32[2,128,128]{2,1,0:T(8,128)} %object_hbm.1, f32[4,256,512]{2,1,0:T(8,128)} %probe_hbm.1, bf16[2,256,256]{2,1,0:T(8,128)(2,1)} %patterns_hbm.1, f32[256,256]{1,0:T(8,128)} %gain_hbm.1, s32[256,256]{1,0:T(8,128)} %mask_hbm.1, ...), custom_call_target="tpu_custom_call" | custom-call | flops 8589934592 | bytes 8388608 | tf_op jit(solution)/shard_map/pallas_call | solution.py:362
  95.1 1.6 %copy.15 = f32[2,128,128]{2,1,0:T(8,128)} copy(f32[2,128,128]{2,1,0:T(8,128)} %get-tuple-element.6) | data formatting | bytes 262144
  96.7 1.2 %copy.16 = f32[2]{0:T(128)} copy(f32[2]{0:T(128)} %get-tuple-element.7) | data formatting | bytes 16
  97.9 1.2 %copy.17 = f32[2,2]{1,0:T(2,128)} copy(f32[2,2]{1,0:T(2,128)} %get-tuple-element.8) | data formatting | bytes 32

commit v3 on v2

--- a/solution.py
+++ b/solution.py
@@ -29,8 +29,8 @@
     object_hbm, probe_hbm, patterns_hbm, gain_hbm, mask_hbm, table_hbm, centres_hbm, live_hbm,
     object_out, steps_out, energies_out,
     probe_ref, patterns_ref, gain_ref, mask_ref, table_ref, centres_ref, live_ref,
-    info, extended, direction_ext, amplitude, power_pad, shifted, coverage, patch, stacked, far, update,
-    deposit, fold, fold_x, fold_y, energy_send, energy_recv, sums_x, sums_y,
+    info, extended, direction_ext, amplitude, power_pad, shifted, coverage, patch, waves, stacked, far, update,
+    deposit, fold, fold_x, fold_y, fold_z, energy_send, energy_recv, sums_x, sums_y,
     load_sem, info_sem, halo_sem, fold_sem, energy_sem, sums_sem,
 ):
     tile = object_hbm.shape[1]
@@ -70,15 +70,11 @@
         pl.semaphore_signal(barrier, inc=1, device_id=at(k, c), device_id_type=MESH)
     pl.semaphore_wait(barrier, len(partners))
 
-    def start_gather(wide, phase):
-        along = []
-        for plane in range(2):
-            mine = wide.at[1, plane, middle, :]
-            along.append(remote(mine, wide.at[1, plane, top, :], halo_sem, (phase, 2 * plane), at(1, 0)))
-            along.append(remote(mine, wide.at[1, plane, bottom, :], halo_sem, (phase, 2 * plane + 1), at(-1, 0)))
-        for copy in along:
-            copy.start()
-        return along, [send_sideways(wide, phase, plane, middle, 4 + 2 * plane) for plane in range(2)]
+    odd = lax.rem(my_obj, 2)
+    near_start = pl.multiple_of(2 * tile * (1 - odd), tile)
+    far_start = pl.multiple_of(2 * tile * odd, tile)
+    near, far_rows = pl.ds(near_start, tile), pl.ds(far_start, tile)
+    pair_step, pass_step = 1 - 2 * odd, 2 - 4 * odd
 
     def send_sideways(wide, phase, plane, rows, first):
         mine = wide.at[1, plane, rows, :]
@@ -90,22 +86,44 @@
             copy.start()
         return pair
 
-    def pass_on(wide, phase, along, beside):
-        beside = list(beside)
-        for n, copy in enumerate(along):
-            copy.wait_recv()
-            beside.append(send_sideways(wide, phase, n // 2, bottom if n % 2 else top, 8 + 2 * n))
-        return beside
-
-    def finish_gather(along, beside):
+    def start_gather(wide, phase):
+        direct = [
+            remote(
+                wide.at[1, plane, middle, :], wide.at[1, plane, far_rows, :],
+                halo_sem, (phase, plane), at(pair_step, 0),
+            )
+            for plane in range(2)
+        ]
+        for copy in direct:
+            copy.start()
+        return direct, [send_sideways(wide, phase, plane, middle, 4 + 2 * plane) for plane in range(2)]
+
+    def pass_near(wide, phase, direct, beside):
+        passed = []
+        for plane in range(2):
+            direct[plane].wait_recv()
+            passed.append(remote(
+                wide.at[1, plane, near, :], wide.at[1, plane, far_rows, :],
+                halo_sem, (phase, 2 + plane), at(pass_step, 0),
+            ))
+            passed[plane].start()
+            beside.append(send_sideways(wide, phase, plane, near, 8 + 2 * plane))
+        return passed
+
+    def pass_far(wide, phase, passed, beside):
+        for plane in range(2):
+            passed[plane].wait_recv()
+            beside.append(send_sideways(wide, phase, plane, far_rows, 12 + 2 * plane))
+
+    def finish_gather(direct, passed, beside):
         for pair in beside:
             for copy in pair:
                 copy.wait()
-        for copy in along:
+        for copy in direct + passed:
             copy.wait_send()
 
     loads[0].wait()
-    along, beside = start_gather(extended, 0)
+    direct, beside = start_gather(extended, 0)
 
     loads[1].wait()
     loads[2].wait()
@@ -143,11 +161,12 @@
                 zeros = jnp.zeros((tile, tile), jnp.float32)
                 deposit[slot, column, plane, :tile, :] = zeros
                 deposit[slot, column, plane, tile + size :, :] = zeros
-    beside = pass_on(extended, 0, along, beside)
+    passed = pass_near(extended, 0, direct, beside)
     loads[7].wait()
 
     for copy in info_copies:
         copy.wait()
+    pass_far(extended, 0, passed, beside)
     lane = lax.broadcasted_iota(jnp.int32, (tile, tile), 1)
     total = jnp.zeros((tile, tile), jnp.float32)
     for n, (k, c) in enumerate(AROUND):
@@ -165,7 +184,7 @@
             shifted[n, slot] = moved
             total = total + moved * alive
     coverage[...] = total
-    finish_gather(along, beside)
+    finish_gather(direct, passed, beside)
 
     wide_lane = lax.broadcasted_iota(jnp.int32, (size, tile), 1)
 
@@ -182,26 +201,30 @@
         for mode in range(modes):
             real, imag = patch[0], patch[1]
             probe_real, probe_imag = probe_ref[mode, :, :size], probe_ref[mode, :, size:]
-            exit_wave = jnp.concatenate(
-                [real * probe_real - imag * probe_imag, real * probe_imag + imag * probe_real], axis=1
-            ).astype(jnp.bfloat16)
-            half = jnp.dot(exit_wave, table_ref[0], preferred_element_type=jnp.float32).astype(jnp.bfloat16)
+            waves[mode, :, :size] = (real * probe_real - imag * probe_imag).astype(jnp.bfloat16)
+            waves[mode, :, size:] = (real * probe_imag + imag * probe_real).astype(jnp.bfloat16)
+        for mode in range(modes):
+            half = jnp.dot(waves[mode], table_ref[0], preferred_element_type=jnp.float32).astype(jnp.bfloat16)
             stacked[mode, :size, :] = half[:, :size]
             stacked[mode, size:, :] = half[:, size:]
+        for mode in range(modes):
             far[mode] = jnp.dot(table_ref[1], stacked[mode], preferred_element_type=jnp.float32)
         model = jnp.zeros((size, size), jnp.float32)
         for mode in range(modes):
             model = model + far[mode, :size, :] ** 2 + far[mode, size:, :] ** 2
         ratio = amplitude[slot] * lax.rsqrt(jnp.maximum(model, 0.25))
+        for mode in range(modes):
+            stacked[mode, :size, :] = (far[mode, :size, :] * ratio).astype(jnp.bfloat16)
+            stacked[mode, size:, :] = (far[mode, size:, :] * ratio).astype(jnp.bfloat16)
+        for mode in range(modes):
+            back = jnp.dot(table_ref[0], stacked[mode], preferred_element_type=jnp.float32).astype(jnp.bfloat16)
+            waves[mode, :, :size] = back[:size]
+            waves[mode, :, size:] = back[size:]
         power = jnp.concatenate([power_pad[half, tile : tile + size, :] for half in range(2)], axis=1)
         update[0] = -power * patch[0]
         update[1] = -power * patch[1]
         for mode in range(modes):
-            stacked[mode, :size, :] = (far[mode, :size, :] * ratio).astype(jnp.bfloat16)
-            stacked[mode, size:, :] = (far[mode, size:, :] * ratio).astype(jnp.bfloat16)
-            back = jnp.dot(table_ref[0], stacked[mode], preferred_element_type=jnp.float32).astype(jnp.bfloat16)
-            back = jnp.concatenate([back[:size], back[size:]], axis=1)
-            wave = jnp.dot(back, table_ref[1], preferred_element_type=jnp.float32)
+            wave = jnp.dot(waves[mode], table_ref[1], preferred_element_type=jnp.float32)
             real, imag = wave[:, :size], wave[:, size:]
             probe_real, probe_imag = probe_ref[mode, :, :size], probe_ref[mode, :, size:]
             update[0] += real * probe_real + imag * probe_imag
@@ -235,64 +258,68 @@
     for iteration in range(ITERS):
         lax.fori_loop(0, slots, one_slot, 0)
 
-        def gathered(column, plane, block):
+        def gathered(column, plane, start):
             summed = None
             for slot in range(slots):
-                rows = pl.ds((block + 1) * tile - centres_ref[slot, 0], tile)
-                term = deposit[slot, column, plane, rows, :]
+                term = deposit[slot, column, plane, pl.ds(start + tile - centres_ref[slot, 0], tile), :]
                 summed = term if summed is None else summed + term
             return summed
 
         sides = {}
-        blocks = (top, middle, bottom)
-        for place, (plane, block) in enumerate(((0, 0), (0, 2), (1, 0), (1, 2), (0, 1), (1, 1))):
-            rows = blocks[block]
+        starts = {"far": far_start, "near": near_start, "middle": tile}
+        for place, (name, plane) in enumerate((name, plane) for name in starts for plane in range(2)):
+            rows = pl.ds(starts[name], tile)
             pair = []
             for side, (column, step) in enumerate(((2, 1), (0, -1))):
-                fold[iteration, column, plane, rows, :] = gathered(column, plane, block)
+                fold[iteration, column, plane, rows, :] = gathered(column, plane, starts[name])
                 copy = remote(
                     fold.at[iteration, column, plane, rows, :], fold_x.at[iteration, side, plane, rows, :],
                     fold_sem, (iteration, 2 * place + side), at(0, step),
                 )
                 copy.start()
                 pair.append(copy)
-            sides[plane, block] = pair
-        for plane in range(2):
-            for block in (0, 2, 1):
-                fold[iteration, 1, plane, blocks[block], :] = gathered(1, plane, block)
-
-        def add_sides(plane, block):
-            rows = blocks[block]
-            for copy in sides[plane, block]:
+            sides[name, plane] = pair
+        for name in starts:
+            for plane in range(2):
+                fold[iteration, 1, plane, pl.ds(starts[name], tile), :] = gathered(1, plane, starts[name])
+
+        def add_sides(name, plane):
+            rows = pl.ds(starts[name], tile)
+            for copy in sides[name, plane]:
                 copy.wait_recv()
             return (
                 fold[iteration, 1, plane, rows, :]
                 + fold_x[iteration, 0, plane, rows, :] + fold_x[iteration, 1, plane, rows, :]
             )
 
-        folds = []
-        for plane in range(2):
-            for side, (block, step) in enumerate(((0, -1), (2, 1))):
-                rows = blocks[block]
-                fold[iteration, 1, plane, rows, :] = add_sides(plane, block)
-                copy = remote(
-                    fold.at[iteration, 1, plane, rows, :], fold_y.at[iteration, side, plane],
-                    fold_sem, (iteration, 12 + 2 * plane + side), at(step, 0),
-                )
-                copy.start()
-                folds.append(copy)
-        own = [add_sides(plane, 1) for plane in range(2)]
+        passed_on, folds = [], []
+        for plane in range(2):
+            fold[iteration, 1, plane, far_rows, :] = add_sides("far", plane)
+            passed_on.append(remote(
+                fold.at[iteration, 1, plane, far_rows, :], fold_z.at[iteration, plane],
+                fold_sem, (iteration, 12 + plane), at(-pass_step, 0),
+            ))
+            passed_on[plane].start()
+        for plane in range(2):
+            total = add_sides("near", plane)
+            passed_on[plane].wait_recv()
+            fold[iteration, 1, plane, near, :] = total + fold_z[iteration, plane]
+            folds.append(remote(
+                fold.at[iteration, 1, plane, near, :], fold_y.at[iteration, plane],
+                fold_sem, (iteration, 14 + plane), at(pair_step, 0),
+            ))
+            folds[plane].start()
+        own = [add_sides("middle", plane) for plane in range(2)]
         cover = coverage[...]
         gradient, moved = [], []
         for plane in range(2):
-            folds[2 * plane].wait_recv()
-            folds[2 * plane + 1].wait_recv()
-            gradient.append(own[plane] + fold_y[iteration, 0, plane] + fold_y[iteration, 1, plane])
+            folds[plane].wait_recv()
+            gradient.append(own[plane] + fold_y[iteration, plane])
             moved.append(gradient[plane] / (cover + 0.5))
             direction_ext[iteration, 1, plane, middle, :] = moved[plane]
         last = iteration == ITERS - 1
         if not last:
-            along, beside = start_gather(direction_ext.at[iteration], 1 + iteration)
+            direct, beside = start_gather(direction_ext.at[iteration], 1 + iteration)
 
         squares = moved[0] * moved[0] + moved[1] * moved[1]
         sums_x[iteration, my_scan] = (
@@ -300,6 +327,8 @@
             + as_row(cover * squares, 1) + jnp.where(row_id == 2, live_number, 0.0)
         )
         first_sums = sum_start(sums_x, my_scan, 0, n_scan, lambda other: at(0, other), iteration)
+        if not last:
+            passed = pass_near(direction_ext.at[iteration], 1 + iteration, direct, beside)
         for n, (k, c) in enumerate(AROUND):
             block = jnp.zeros((8, tile), jnp.float32)
             for slot in range(slots):
@@ -319,11 +348,11 @@
         sums_y[iteration, my_obj] = jnp.sum(sums_x[iteration], axis=0)
         second_sums = sum_start(sums_y, my_obj, n_scan, n_obj, lambda other: at(other, 0), iteration)
         if not last:
-            beside = pass_on(direction_ext.at[iteration], 1 + iteration, along, beside)
+            pass_far(direction_ext.at[iteration], 1 + iteration, passed, beside)
         for pair in sides.values():
             for copy in pair:
                 copy.wait_send()
-        for copy in folds:
+        for copy in folds + passed_on:
             copy.wait_send()
         for copy in second_sums:
             copy.wait()
@@ -332,7 +361,7 @@
         step = rows[0:1] / rows[1:2]
         scales.append((step, rows[2:3] * (1.0 / tile) / rows[1:2]))
         if not last:
-            finish_gather(along, beside)
+            finish_gather(direct, passed, beside)
             extended[...] = extended[...] + step.reshape(1, 1, 1, 1) * direction_ext[iteration]
         else:
             object_out[...] = (
@@ -384,13 +413,15 @@
             pltpu.VMEM((9, slots, tile, tile), f32),
             pltpu.VMEM((tile, tile), f32),
             pltpu.VMEM((2, size, size), f32),
+            pltpu.VMEM((modes, size, 2 * size), jnp.bfloat16),
             pltpu.VMEM((modes, 2 * size, size), jnp.bfloat16),
             pltpu.VMEM((modes, 2 * size, size), f32),
             pltpu.VMEM((2, size, size), f32),
             pltpu.VMEM((slots, 3, 2, size + 2 * tile, tile), f32),
             pltpu.VMEM((ITERS, 3, 2, extent, tile), f32),
             pltpu.VMEM((ITERS, 2, 2, extent, tile), f32),
-            pltpu.VMEM((ITERS, 2, 2, tile, tile), f32),
+            pltpu.VMEM((ITERS, 2, tile, tile), f32),
+            pltpu.VMEM((ITERS, 2, tile, tile), f32),
             pltpu.VMEM((ITERS, 9, 8, tile), f32),
             pltpu.VMEM((ITERS, 9, 8, tile), f32),
             pltpu.VMEM((ITERS, n_scan, 8, tile), f32),
@@ -403,7 +434,7 @@
             pltpu.SemaphoreType.DMA((2, ITERS, n_scan + n_obj)),
         ],
         compiler_params=pltpu.CompilerParams(
-            collective_id=0, has_side_effects=True, vmem_limit_bytes=62 * 1024 * 1024
+            collective_id=0, has_side_effects=True, vmem_limit_bytes=55000 * 1024
         ),
         cost_estimate=pl.CostEstimate(flops=flops, bytes_accessed=8 * 1024 * 1024, transcendentals=0),
     )(object_field, probe_modes, patterns, gain_map, defect_mask, table, probe_centres, live_counts)

time: 99.2 us -> 91 us (0.917)
  Pallas kernels: 93.8 us -> 87.2 us
  local copies, waits for them, and re-layouts: 3.96 us -> 2.4 us
    pallas_call x1, Pallas kernels: 93.8 us -> 87.2 us  [on_device(): pl.pallas_call(functools.partial(kernel, n_scan, n_obj), out_shape=(jax.S...]
    unnamed x3 -> x5, local copies, waits for them, and re-layouts: 3.96 us -> 2.4 us
where the time goes in v3:
time: 91 us; the launch traced here: 90.9 us
  Pallas kernels  87.2 us (96%)
  local copies, waits for them, and re-layouts  2.4 us (3%)
  between operations  1.3 us (1%)
    pallas_call x1, Pallas kernels, on_device(): pl.pallas_call(functools.partial(kernel, n_scan, n_obj), out_shape=(jax.S...  87.2 us
    unnamed x5, local copies, waits for them, and re-layouts  2.4 us

profile of v3, /device:TPU:1, one launch (start us, length us, event | category | flops | bytes accessed | tf_op | source)
XLA Modules:
  0.0 90.9 jit_solution(5458276181629867651)
XLA Ops:
  1.3 0.0 copy-start
  1.3 0.7 copy-done
  2.0 87.2 %shard_map.103 = (f32[2,128,128]{2,1,0:T(8,128)S(1)}, f32[2]{0:T(128)S(1)}, f32[2,2]{1,0:T(2,128)S(1)}) custom-call(f32[2,128,128]{2,1,0:T(8,128)} %object_hbm.1, f32[4,256,512]{2,1,0:T(8,128)} %probe_hbm.1, bf16[2,256,256]{2,1,0:T(8,128)(2,1)} %patterns_hbm.1, f32[256,256]{1,0:T(8,128)} %gain_hbm.1, s32[256,256]{1,0:T(8,128)} %mask_hbm.1, ...), custom_call_target="tpu_custom_call" | custom-call | flops 8589934592 | bytes 8388608 | tf_op jit(solution)/shard_map/pallas_call | solution.py:391
  89.1 0.7 copy.15
  89.8 0.5 copy.16
  90.3 0.6 copy.17
Async XLA Ops:
  1.3 0.7 copy-start

commit v4 on v3

--- a/solution.py
+++ b/solution.py
@@ -19,9 +19,14 @@
     angles = phase * np.float32(2.0 * 3.141592653589793 / size)
     norm = np.float32(size ** (-0.5))
     cosine, sine = np.cos(angles) * norm, np.sin(angles) * norm
-    first = np.block([[cosine, -sine], [sine, cosine]])
-    second = np.block([[cosine, sine], [-sine, cosine]])
-    return jnp.asarray(np.stack([first, second])).astype(jnp.bfloat16)
+    tables = []
+    for first in range(2):
+        c, s = cosine[: size // 2, first::2], sine[: size // 2, first::2]
+        tables.append(np.block([[c, -s], [s, c]]))
+    for first in range(2):
+        c, s = cosine[first::2, : size // 2], sine[first::2, : size // 2]
+        tables.append(np.block([[c, s], [-s, c]]))
+    return jnp.asarray(np.stack(tables)).astype(jnp.bfloat16)
 
 
 def kernel(
@@ -164,6 +169,16 @@
     passed = pass_near(extended, 0, direct, beside)
     loads[7].wait()
 
+    place = lax.broadcasted_iota(jnp.int32, (size, size), 0)
+    taken = lax.broadcasted_iota(jnp.int32, (size, size), 1)
+    half_size = size // 2
+    by_row = jnp.where(place < half_size, 2 * place, 2 * place - (size - 1)) == taken
+    by_column = jnp.where(taken < half_size, 2 * taken, 2 * taken - (size - 1)) == place
+    by_row, by_column = by_row.astype(jnp.float32), by_column.astype(jnp.float32)
+    for slot in range(slots):
+        ordered = jnp.dot(amplitude[slot], by_column, precision=lax.Precision.HIGHEST)
+        amplitude[slot] = jnp.dot(by_row, ordered, precision=lax.Precision.HIGHEST)
+
     for copy in info_copies:
         copy.wait()
     pass_far(extended, 0, passed, beside)
@@ -188,56 +203,98 @@
 
     wide_lane = lax.broadcasted_iota(jnp.int32, (size, tile), 1)
 
-    def one_slot(slot, carry):
+    def product(left, right):
+        return jnp.dot(left, right, preferred_element_type=jnp.float32)
+
+    def take_patch(slot):
         row, column = centres_ref[slot, 0], centres_ref[slot, 1]
         back_shift = lax.rem(tile - column, tile)
-        near = wide_lane < tile - column
+        close = wide_lane < tile - column
         for plane in range(2):
             first, second, third = (
                 pltpu.roll(extended[block, plane, pl.ds(row, size), :], back_shift, 1) for block in range(3)
             )
-            patch[plane, :, :tile] = jnp.where(near, first, second)
-            patch[plane, :, tile:] = jnp.where(near, second, third)
+            patch[slot, plane, :, :tile] = jnp.where(close, first, second)
+            patch[slot, plane, :, tile:] = jnp.where(close, second, third)
+
+    def exit_waves(slot):
         for mode in range(modes):
-            real, imag = patch[0], patch[1]
+            real, imag = patch[slot, 0], patch[slot, 1]
             probe_real, probe_imag = probe_ref[mode, :, :size], probe_ref[mode, :, size:]
-            waves[mode, :, :size] = (real * probe_real - imag * probe_imag).astype(jnp.bfloat16)
-            waves[mode, :, size:] = (real * probe_imag + imag * probe_real).astype(jnp.bfloat16)
+            for part, wave in enumerate((real * probe_real - imag * probe_imag, real * probe_imag + imag * probe_real)):
+                low, high = wave[:, :tile], wave[:, tile:]
+                first = part * tile
+                waves[slot, mode, :, first : first + tile] = (low + high).astype(jnp.bfloat16)
+                waves[slot, mode, :, size + first : size + first + tile] = (low - high).astype(jnp.bfloat16)
+
+    def along_columns(slot):
         for mode in range(modes):
-            half = jnp.dot(waves[mode], table_ref[0], preferred_element_type=jnp.float32).astype(jnp.bfloat16)
-            stacked[mode, :size, :] = half[:, :size]
-            stacked[mode, size:, :] = half[:, size:]
+            for parity in range(2):
+                half = product(waves[slot, mode, :, parity * size : (parity + 1) * size], table_ref[parity])
+                lanes = slice(parity * tile, (parity + 1) * tile)
+                for place, value in enumerate((half[:tile] + half[tile:], half[:tile] - half[tile:])):
+                    value = value.astype(jnp.bfloat16)
+                    stacked[slot, mode, place * size : place * size + tile, lanes] = value[:, :tile]
+                    stacked[slot, mode, place * size + tile : (place + 1) * size, lanes] = value[:, tile:]
+
+    def along_rows(slot):
         for mode in range(modes):
-            far[mode] = jnp.dot(table_ref[1], stacked[mode], preferred_element_type=jnp.float32)
-        model = jnp.zeros((size, size), jnp.float32)
+            for parity in range(2):
+                rows = slice(parity * size, (parity + 1) * size)
+                far[slot, mode, rows, :] = product(table_ref[2 + parity], stacked[slot, mode, rows, :])
+
+    def revise(slot):
+        for parity in range(2):
+            parts = [slice(parity * size + part * tile, parity * size + (part + 1) * tile) for part in range(2)]
+            model = jnp.zeros((tile, size), jnp.float32)
+            for mode in range(modes):
+                model = model + far[slot, mode, parts[0], :] ** 2 + far[slot, mode, parts[1], :] ** 2
+            ratio = amplitude[slot, parity * tile : (parity + 1) * tile, :] * lax.rsqrt(jnp.maximum(model, 0.25))
+            for mode in range(modes):
+                for part in parts:
+                    stacked[slot, mode, part, :] = (far[slot, mode, part, :] * ratio).astype(jnp.bfloat16)
+
+    def back_along_rows(slot):
         for mode in range(modes):
-            model = model + far[mode, :size, :] ** 2 + far[mode, size:, :] ** 2
-        ratio = amplitude[slot] * lax.rsqrt(jnp.maximum(model, 0.25))
+            even = product(table_ref[0], stacked[slot, mode, :size, :])
+            odd = product(table_ref[1], stacked[slot, mode, size:, :])
+            for rows, value in ((slice(0, tile), even + odd), (slice(tile, size), even - odd)):
+                value = value.astype(jnp.bfloat16)
+                for parity in range(2):
+                    lanes = slice(parity * tile, (parity + 1) * tile)
+                    waves[slot, mode, rows, parity * size : parity * size + tile] = value[:tile, lanes]
+                    waves[slot, mode, rows, parity * size + tile : (parity + 1) * size] = value[tile:, lanes]
+
+    def back_along_columns(slot):
+        for plane in range(2):
+            for half in range(2):
+                lanes = slice(half * tile, (half + 1) * tile)
+                update[slot, plane, :, lanes] = -power_pad[half, tile : tile + size, :] * patch[slot, plane, :, lanes]
         for mode in range(modes):
-            stacked[mode, :size, :] = (far[mode, :size, :] * ratio).astype(jnp.bfloat16)
-            stacked[mode, size:, :] = (far[mode, size:, :] * ratio).astype(jnp.bfloat16)
-        for mode in range(modes):
-            back = jnp.dot(table_ref[0], stacked[mode], preferred_element_type=jnp.float32).astype(jnp.bfloat16)
-            waves[mode, :, :size] = back[:size]
-            waves[mode, :, size:] = back[size:]
-        power = jnp.concatenate([power_pad[half, tile : tile + size, :] for half in range(2)], axis=1)
-        update[0] = -power * patch[0]
-        update[1] = -power * patch[1]
-        for mode in range(modes):
-            wave = jnp.dot(waves[mode], table_ref[1], preferred_element_type=jnp.float32)
-            real, imag = wave[:, :size], wave[:, size:]
-            probe_real, probe_imag = probe_ref[mode, :, :size], probe_ref[mode, :, size:]
-            update[0] += real * probe_real + imag * probe_imag
-            update[1] += imag * probe_real - real * probe_imag
-        alive = (slot < live_ref[0]).astype(jnp.float32)
-        far_lane = wide_lane < column
-        for plane in range(2):
-            low = pltpu.roll(update[plane, :, :tile] * alive, column, 1)
-            high = pltpu.roll(update[plane, :, tile:] * alive, column, 1)
-            deposit[slot, 0, plane, tile : tile + size, :] = jnp.where(far_lane, 0.0, low)
-            deposit[slot, 1, plane, tile : tile + size, :] = jnp.where(far_lane, low, high)
-            deposit[slot, 2, plane, tile : tile + size, :] = jnp.where(far_lane, high, 0.0)
-        return carry
+            even = product(waves[slot, mode, :, :size], table_ref[2])
+            odd = product(waves[slot, mode, :, size:], table_ref[3])
+            for half, wave in enumerate((even + odd, even - odd)):
+                real, imag = wave[:, :tile], wave[:, tile:]
+                lanes = slice(half * tile, (half + 1) * tile)
+                probe_real = probe_ref[mode, :, lanes]
+                probe_imag = probe_ref[mode, :, size + half * tile : size + (half + 1) * tile]
+                update[slot, 0, :, lanes] += real * probe_real + imag * probe_imag
+                update[slot, 1, :, lanes] += imag * probe_real - real * probe_imag
+
+    def put_deposit(slot):
+        column = centres_ref[slot, 1]
+        alive = jnp.where(slot < live_ref[0], 1.0, 0.0)
+        before = wide_lane < column
+        for plane in range(2):
+            low = pltpu.roll(update[slot, plane, :, :tile] * alive, column, 1)
+            high = pltpu.roll(update[slot, plane, :, tile:] * alive, column, 1)
+            deposit[slot, 0, plane, tile : tile + size, :] = jnp.where(before, 0.0, low)
+            deposit[slot, 1, plane, tile : tile + size, :] = jnp.where(before, low, high)
+            deposit[slot, 2, plane, tile : tile + size, :] = jnp.where(before, high, 0.0)
+
+    stages = (
+        take_patch, exit_waves, along_columns, along_rows, revise, back_along_rows, back_along_columns, put_deposit
+    )
 
     row_id = lax.broadcasted_iota(jnp.int32, (8, tile), 0)
 
@@ -256,7 +313,9 @@
 
     energy_copies, scales = [], []
     for iteration in range(ITERS):
-        lax.fori_loop(0, slots, one_slot, 0)
+        for stage in stages:
+            for slot in range(slots):
+                stage(slot)
 
         def gathered(column, plane, start):
             summed = None
@@ -387,7 +446,7 @@
     f32 = jnp.float32
     vmem, smem = pl.BlockSpec(memory_space=pltpu.VMEM), pl.BlockSpec(memory_space=pltpu.SMEM)
     hbm = pl.BlockSpec(memory_space=pltpu.HBM)
-    flops = ITERS * slots * modes * 4 * 2 * size * (2 * size) ** 2
+    flops = ITERS * slots * modes * 4 * 2 * (2 * size) * size * size
     outputs = pl.pallas_call(
         functools.partial(kernel, n_scan, n_obj),
         out_shape=(
@@ -412,11 +471,11 @@
             pltpu.VMEM((2, size + 2 * tile, tile), f32),
             pltpu.VMEM((9, slots, tile, tile), f32),
             pltpu.VMEM((tile, tile), f32),
-            pltpu.VMEM((2, size, size), f32),
-            pltpu.VMEM((modes, size, 2 * size), jnp.bfloat16),
-            pltpu.VMEM((modes, 2 * size, size), jnp.bfloat16),
-            pltpu.VMEM((modes, 2 * size, size), f32),
-            pltpu.VMEM((2, size, size), f32),
+            pltpu.VMEM((slots, 2, size, size), f32),
+            pltpu.VMEM((slots, modes, size, 2 * size), jnp.bfloat16),
+            pltpu.VMEM((slots, modes, 2 * size, size), jnp.bfloat16),
+            pltpu.VMEM((slots, modes, 2 * size, size), f32),
+            pltpu.VMEM((slots, 2, size, size), f32),
             pltpu.VMEM((slots, 3, 2, size + 2 * tile, tile), f32),
             pltpu.VMEM((ITERS, 3, 2, extent, tile), f32),
             pltpu.VMEM((ITERS, 2, 2, extent, tile), f32),

time: 91 us -> 86.9 us (0.955)
  Pallas kernels: 87.2 us -> 83 us
    pallas_call x1, Pallas kernels: 87.2 us -> 83 us  [on_device(): pl.pallas_call(functools.partial(kernel, n_scan, n_obj), out_shape=(jax.S...]
where the time goes in v4:
time: 86.9 us; the launch traced here: 86.7 us
  Pallas kernels  83 us (96%)
  local copies, waits for them, and re-layouts  2.4 us (3%)
  between operations  1.3 us (1%)
    pallas_call x1, Pallas kernels, on_device(): pl.pallas_call(functools.partial(kernel, n_scan, n_obj), out_shape=(jax.S...  83 us
    unnamed x5, local copies, waits for them, and re-layouts  2.4 us

profile of v4, /device:TPU:1, one launch (start us, length us, event | category | flops | bytes accessed | tf_op | source)
XLA Modules:
  0.0 86.7 jit_solution(225369739937401053)
XLA Ops:
  1.3 0.0 copy-start
  1.3 0.7 copy-done
  2.0 83.0 %shard_map.103 = (f32[2,128,128]{2,1,0:T(8,128)S(1)}, f32[2]{0:T(128)S(1)}, f32[2,2]{1,0:T(2,128)S(1)}) custom-call(f32[2,128,128]{2,1,0:T(8,128)} %object_hbm.1, f32[4,256,512]{2,1,0:T(8,128)} %probe_hbm.1, bf16[2,256,256]{2,1,0:T(8,128)(2,1)} %patterns_hbm.1, f32[256,256]{1,0:T(8,128)} %gain_hbm.1, s32[256,256]{1,0:T(8,128)} %mask_hbm.1, ...), custom_call_target="tpu_custom_call" | custom-call | flops 4294967296 | bytes 8388608 | tf_op jit(solution)/shard_map/pallas_call | solution.py:450
  85.0 0.7 copy.15
  85.7 0.5 copy.16
  86.2 0.6 copy.17
Async XLA Ops:
  1.3 0.7 copy-start

commit v5 on v4

--- a/solution.py
+++ b/solution.py
@@ -35,7 +35,7 @@
     object_out, steps_out, energies_out,
     probe_ref, patterns_ref, gain_ref, mask_ref, table_ref, centres_ref, live_ref,
     info, extended, direction_ext, amplitude, power_pad, shifted, coverage, patch, waves, stacked, far, update,
-    deposit, fold, fold_x, fold_y, fold_z, energy_send, energy_recv, sums_x, sums_y,
+    deposit, fold, fold_x, fold_y, fold_z, corner_y, corner_z, energy_send, energy_recv, sums_x, sums_y,
     load_sem, info_sem, halo_sem, fold_sem, energy_sem, sums_sem,
 ):
     tile = object_hbm.shape[1]
@@ -81,54 +81,107 @@
     near, far_rows = pl.ds(near_start, tile), pl.ds(far_start, tile)
     pair_step, pass_step = 1 - 2 * odd, 2 - 4 * odd
 
-    def send_sideways(wide, phase, plane, rows, first):
+    run = n_scan // 2
+    turn_right, turn_left = lax.rem(my_scan, run) == run - 1, lax.rem(my_scan, run) == 0
+    on_right, on_left = jnp.logical_not(turn_right), jnp.logical_not(turn_left)
+    turns = ((2, 1, turn_right), (0, -1, turn_left))
+
+    def when(condition, act):
+        if condition is None:
+            act()
+        else:
+            pl.when(condition)(act)
+
+    class Copy:
+        def __init__(self, copy, sends=None, receives=None):
+            self.start = lambda: when(sends, copy.start)
+            self.wait_send = lambda: when(sends, copy.wait_send)
+            self.wait_recv = lambda: when(receives, copy.wait_recv)
+
+        def wait(self):
+            self.wait_recv()
+            self.wait_send()
+
+    def send_sideways(wide, phase, plane, rows, first, corner):
         mine = wide.at[1, plane, rows, :]
         pair = (
-            remote(mine, wide.at[0, plane, rows, :], halo_sem, (phase, first), at(0, 1)),
-            remote(mine, wide.at[2, plane, rows, :], halo_sem, (phase, first + 1), at(0, -1)),
+            Copy(
+                remote(mine, wide.at[0, plane, rows, :], halo_sem, (phase, first), at(0, 1)),
+                *((on_right, on_left) if corner else ()),
+            ),
+            Copy(
+                remote(mine, wide.at[2, plane, rows, :], halo_sem, (phase, first + 1), at(0, -1)),
+                *((on_left, on_right) if corner else ()),
+            ),
         )
         for copy in pair:
             copy.start()
         return pair
 
     def start_gather(wide, phase):
-        direct = [
-            remote(
-                wide.at[1, plane, middle, :], wide.at[1, plane, far_rows, :],
-                halo_sem, (phase, plane), at(pair_step, 0),
-            )
-            for plane in range(2)
-        ]
-        for copy in direct:
-            copy.start()
-        return direct, [send_sideways(wide, phase, plane, middle, 4 + 2 * plane) for plane in range(2)]
-
-    def pass_near(wide, phase, direct, beside):
+        direct, corners = [], []
+        for plane in range(2):
+            mine = wide.at[1, plane, middle, :]
+            direct.append(remote(
+                mine, wide.at[1, plane, far_rows, :], halo_sem, (phase, plane), at(pair_step, 0)
+            ))
+            direct[plane].start()
+            corners.append([
+                Copy(
+                    remote(
+                        mine, wide.at[2 - column, plane, far_rows, :],
+                        halo_sem, (phase, 16 + 2 * plane + side), at(pair_step, step),
+                    ),
+                    turn, turns[1 - side][2],
+                )
+                for side, (column, step, turn) in enumerate(turns)
+            ])
+            for copy in corners[plane]:
+                copy.start()
+        beside = [send_sideways(wide, phase, plane, middle, 4 + 2 * plane, False) for plane in range(2)]
+        return direct, corners, beside
+
+    def pass_near(wide, phase, state):
+        direct, corners, beside = state
         passed = []
         for plane in range(2):
             direct[plane].wait_recv()
-            passed.append(remote(
+            passed.append(Copy(remote(
                 wide.at[1, plane, near, :], wide.at[1, plane, far_rows, :],
                 halo_sem, (phase, 2 + plane), at(pass_step, 0),
-            ))
-            passed[plane].start()
-            beside.append(send_sideways(wide, phase, plane, near, 8 + 2 * plane))
+            )))
+            passed[-1].start()
+            beside.append(send_sideways(wide, phase, plane, near, 8 + 2 * plane, True))
+        for plane in range(2):
+            for side, (column, step, turn) in enumerate(turns):
+                corners[plane][1 - side].wait_recv()
+                passed.append(Copy(
+                    remote(
+                        wide.at[column, plane, near, :], wide.at[column, plane, far_rows, :],
+                        halo_sem, (phase, 20 + 2 * plane + side), at(pass_step, 0),
+                    ),
+                    turn, turn,
+                ))
+                passed[-1].start()
         return passed
 
-    def pass_far(wide, phase, passed, beside):
+    def pass_far(wide, phase, state, passed):
         for plane in range(2):
             passed[plane].wait_recv()
-            beside.append(send_sideways(wide, phase, plane, far_rows, 12 + 2 * plane))
-
-    def finish_gather(direct, passed, beside):
+            state[2].append(send_sideways(wide, phase, plane, far_rows, 12 + 2 * plane, True))
+
+    def finish_gather(state, passed):
+        direct, corners, beside = state
         for pair in beside:
             for copy in pair:
                 copy.wait()
-        for copy in direct + passed:
+        for copy in passed[2:]:
+            copy.wait_recv()
+        for copy in direct + passed + corners[0] + corners[1]:
             copy.wait_send()
 
     loads[0].wait()
-    direct, beside = start_gather(extended, 0)
+    state = start_gather(extended, 0)
 
     loads[1].wait()
     loads[2].wait()
@@ -166,7 +219,7 @@
                 zeros = jnp.zeros((tile, tile), jnp.float32)
                 deposit[slot, column, plane, :tile, :] = zeros
                 deposit[slot, column, plane, tile + size :, :] = zeros
-    passed = pass_near(extended, 0, direct, beside)
+    passed = pass_near(extended, 0, state)
     loads[7].wait()
 
     place = lax.broadcasted_iota(jnp.int32, (size, size), 0)
@@ -181,7 +234,7 @@
 
     for copy in info_copies:
         copy.wait()
-    pass_far(extended, 0, passed, beside)
+    pass_far(extended, 0, state, passed)
     lane = lax.broadcasted_iota(jnp.int32, (tile, tile), 1)
     total = jnp.zeros((tile, tile), jnp.float32)
     for n, (k, c) in enumerate(AROUND):
@@ -199,7 +252,7 @@
             shifted[n, slot] = moved
             total = total + moved * alive
     coverage[...] = total
-    finish_gather(direct, passed, beside)
+    finish_gather(state, passed)
 
     wide_lane = lax.broadcasted_iota(jnp.int32, (size, tile), 1)
 
@@ -324,16 +377,28 @@
                 summed = term if summed is None else summed + term
             return summed
 
-        sides = {}
+        sides, corners = {}, []
         starts = {"far": far_start, "near": near_start, "middle": tile}
         for place, (name, plane) in enumerate((name, plane) for name in starts for plane in range(2)):
             rows = pl.ds(starts[name], tile)
             pair = []
-            for side, (column, step) in enumerate(((2, 1), (0, -1))):
+            for side, (column, step, turn) in enumerate(turns):
                 fold[iteration, column, plane, rows, :] = gathered(column, plane, starts[name])
-                copy = remote(
-                    fold.at[iteration, column, plane, rows, :], fold_x.at[iteration, side, plane, rows, :],
-                    fold_sem, (iteration, 2 * place + side), at(0, step),
+                if name == "far":
+                    corners.append(Copy(
+                        remote(
+                            fold.at[iteration, column, plane, rows, :], corner_z.at[iteration, side, plane],
+                            fold_sem, (iteration, 16 + 2 * plane + side), at(-pass_step, 0),
+                        ),
+                        turn, turn,
+                    ))
+                    corners[-1].start()
+                copy = Copy(
+                    remote(
+                        fold.at[iteration, column, plane, rows, :], fold_x.at[iteration, side, plane, rows, :],
+                        fold_sem, (iteration, 2 * place + side), at(0, step),
+                    ),
+                    *(() if name == "middle" else ((on_right, on_left), (on_left, on_right))[side]),
                 )
                 copy.start()
                 pair.append(copy)
@@ -344,41 +409,64 @@
 
         def add_sides(name, plane):
             rows = pl.ds(starts[name], tile)
-            for copy in sides[name, plane]:
+            for side, copy in enumerate(sides[name, plane]):
+                def add(side=side):
+                    fold[iteration, 1, plane, rows, :] += fold_x[iteration, side, plane, rows, :]
+
                 copy.wait_recv()
-            return (
-                fold[iteration, 1, plane, rows, :]
-                + fold_x[iteration, 0, plane, rows, :] + fold_x[iteration, 1, plane, rows, :]
-            )
-
-        passed_on, folds = [], []
-        for plane in range(2):
-            fold[iteration, 1, plane, far_rows, :] = add_sides("far", plane)
+                when(None if name == "middle" else (on_left, on_right)[side], add)
+
+        passed_on, folds, straight = [], [], []
+        for plane in range(2):
+            add_sides("far", plane)
             passed_on.append(remote(
                 fold.at[iteration, 1, plane, far_rows, :], fold_z.at[iteration, plane],
                 fold_sem, (iteration, 12 + plane), at(-pass_step, 0),
             ))
             passed_on[plane].start()
         for plane in range(2):
-            total = add_sides("near", plane)
+            for side, (column, step, turn) in enumerate(turns):
+                def add_corner(plane=plane, side=side, column=column):
+                    fold[iteration, column, plane, near, :] += corner_z[iteration, side, plane]
+
+                corners[2 * plane + side].wait_recv()
+                when(turn, add_corner)
+                straight.append(Copy(
+                    remote(
+                        fold.at[iteration, column, plane, near, :], corner_y.at[iteration, side, plane],
+                        fold_sem, (iteration, 20 + 2 * plane + side), at(pair_step, step),
+                    ),
+                    turn, turns[1 - side][2],
+                ))
+                straight[-1].start()
+        for plane in range(2):
+            add_sides("near", plane)
             passed_on[plane].wait_recv()
-            fold[iteration, 1, plane, near, :] = total + fold_z[iteration, plane]
+            fold[iteration, 1, plane, near, :] += fold_z[iteration, plane]
             folds.append(remote(
                 fold.at[iteration, 1, plane, near, :], fold_y.at[iteration, plane],
                 fold_sem, (iteration, 14 + plane), at(pair_step, 0),
             ))
             folds[plane].start()
-        own = [add_sides("middle", plane) for plane in range(2)]
+        for plane in range(2):
+            add_sides("middle", plane)
+        for plane in range(2):
+            for side in range(2):
+                def add_straight(plane=plane, side=side):
+                    fold[iteration, 1, plane, middle, :] += corner_y[iteration, side, plane]
+
+                straight[2 * plane + side].wait_recv()
+                when(turns[1 - side][2], add_straight)
         cover = coverage[...]
         gradient, moved = [], []
         for plane in range(2):
             folds[plane].wait_recv()
-            gradient.append(own[plane] + fold_y[iteration, plane])
+            gradient.append(fold[iteration, 1, plane, middle, :] + fold_y[iteration, plane])
             moved.append(gradient[plane] / (cover + 0.5))
             direction_ext[iteration, 1, plane, middle, :] = moved[plane]
         last = iteration == ITERS - 1
         if not last:
-            direct, beside = start_gather(direction_ext.at[iteration], 1 + iteration)
+            state = start_gather(direction_ext.at[iteration], 1 + iteration)
 
         squares = moved[0] * moved[0] + moved[1] * moved[1]
         sums_x[iteration, my_scan] = (
@@ -387,7 +475,7 @@
         )
         first_sums = sum_start(sums_x, my_scan, 0, n_scan, lambda other: at(0, other), iteration)
         if not last:
-            passed = pass_near(direction_ext.at[iteration], 1 + iteration, direct, beside)
+            passed = pass_near(direction_ext.at[iteration], 1 + iteration, state)
         for n, (k, c) in enumerate(AROUND):
             block = jnp.zeros((8, tile), jnp.float32)
             for slot in range(slots):
@@ -407,11 +495,11 @@
         sums_y[iteration, my_obj] = jnp.sum(sums_x[iteration], axis=0)
         second_sums = sum_start(sums_y, my_obj, n_scan, n_obj, lambda other: at(other, 0), iteration)
         if not last:
-            pass_far(direction_ext.at[iteration], 1 + iteration, passed, beside)
+            pass_far(direction_ext.at[iteration], 1 + iteration, state, passed)
         for pair in sides.values():
             for copy in pair:
                 copy.wait_send()
-        for copy in folds + passed_on:
+        for copy in folds + passed_on + corners + straight:
             copy.wait_send()
         for copy in second_sums:
             copy.wait()
@@ -420,7 +508,7 @@
         step = rows[0:1] / rows[1:2]
         scales.append((step, rows[2:3] * (1.0 / tile) / rows[1:2]))
         if not last:
-            finish_gather(direct, passed, beside)
+            finish_gather(state, passed)
             extended[...] = extended[...] + step.reshape(1, 1, 1, 1) * direction_ext[iteration]
         else:
             object_out[...] = (
@@ -481,14 +569,16 @@
             pltpu.VMEM((ITERS, 2, 2, extent, tile), f32),
             pltpu.VMEM((ITERS, 2, tile, tile), f32),
             pltpu.VMEM((ITERS, 2, tile, tile), f32),
+            pltpu.VMEM((ITERS, 2, 2, tile, tile), f32),
+            pltpu.VMEM((ITERS, 2, 2, tile, tile), f32),
             pltpu.VMEM((ITERS, 9, 8, tile), f32),
             pltpu.VMEM((ITERS, 9, 8, tile), f32),
             pltpu.VMEM((ITERS, n_scan, 8, tile), f32),
             pltpu.VMEM((ITERS, n_obj, 8, tile), f32),
             pltpu.SemaphoreType.DMA((8,)),
             pltpu.SemaphoreType.DMA((2, 9)),
-            pltpu.SemaphoreType.DMA((2, ITERS, 16)),
-            pltpu.SemaphoreType.DMA((2, ITERS, 16)),
+            pltpu.SemaphoreType.DMA((2, ITERS, 24)),
+            pltpu.SemaphoreType.DMA((2, ITERS, 24)),
             pltpu.SemaphoreType.DMA((2, ITERS, 9)),
             pltpu.SemaphoreType.DMA((2, ITERS, n_scan + n_obj)),
         ],

time: 86.9 us -> 84.1 us (0.968)
  Pallas kernels: 83 us -> 80.2 us
    pallas_call x1, Pallas kernels: 83 us -> 80.2 us  [on_device(): pl.pallas_call(functools.partial(kernel, n_scan, n_obj), out_shape=(jax.S...]
where the time goes in v5:
time: 84.1 us; the launch traced here: 83.9 us
  Pallas kernels  80.2 us (95%)
  local copies, waits for them, and re-layouts  2.4 us (3%)
  between operations  1.3 us (2%)
    pallas_call x1, Pallas kernels, on_device(): pl.pallas_call(functools.partial(kernel, n_scan, n_obj), out_shape=(jax.S...  80.2 us
    unnamed x5, local copies, waits for them, and re-layouts  2.4 us

profile of v5, /device:TPU:1, one launch (start us, length us, event | category | flops | bytes accessed | tf_op | source)
XLA Modules:
  0.0 83.9 jit_solution(5944982203865204816)
XLA Ops:
  1.3 0.0 copy-start
  1.3 0.7 copy-done
  2.0 80.2 %shard_map.103 = (f32[2,128,128]{2,1,0:T(8,128)S(1)}, f32[2]{0:T(128)S(1)}, f32[2,2]{1,0:T(2,128)S(1)}) custom-call(f32[2,128,128]{2,1,0:T(8,128)} %object_hbm.1, f32[4,256,512]{2,1,0:T(8,128)} %probe_hbm.1, bf16[2,256,256]{2,1,0:T(8,128)(2,1)} %patterns_hbm.1, f32[256,256]{1,0:T(8,128)} %gain_hbm.1, s32[256,256]{1,0:T(8,128)} %mask_hbm.1, ...), custom_call_target="tpu_custom_call" | custom-call | flops 4294967296 | bytes 8388608 | tf_op jit(solution)/shard_map/pallas_call | solution.py:538
  82.2 0.7 copy.15
  82.9 0.5 copy.16
  83.4 0.6 copy.17
Async XLA Ops:
  1.3 0.7 copy-start

commit v6 on v5

--- a/solution.py
+++ b/solution.py
@@ -9,6 +9,7 @@
 from jax.sharding import PartitionSpec as P
 
 ITERS = 2
+PARTS = 2
 MESH = pl.DeviceIdType.MESH
 AROUND = [(k, c) for k in (-1, 0, 1) for c in (-1, 0, 1)]
 
@@ -118,47 +119,55 @@
             copy.start()
         return pair
 
+    depth = tile // PARTS
+    pieces = [(plane, part) for plane in range(2) for part in range(PARTS)]
+    count = len(pieces)
+
+    def piece_rows(start, part):
+        return pl.ds(pl.multiple_of(start + part * depth, depth), depth)
+
     def start_gather(wide, phase):
         direct, corners = [], []
-        for plane in range(2):
-            mine = wide.at[1, plane, middle, :]
-            direct.append(remote(
-                mine, wide.at[1, plane, far_rows, :], halo_sem, (phase, plane), at(pair_step, 0)
-            ))
-            direct[plane].start()
+        for n, (plane, part) in enumerate(pieces):
+            mine = wide.at[1, plane, piece_rows(tile, part), :]
+            there = piece_rows(far_start, part)
+            direct.append(remote(mine, wide.at[1, plane, there, :], halo_sem, (phase, n), at(pair_step, 0)))
+            direct[n].start()
             corners.append([
                 Copy(
                     remote(
-                        mine, wide.at[2 - column, plane, far_rows, :],
-                        halo_sem, (phase, 16 + 2 * plane + side), at(pair_step, step),
+                        mine, wide.at[2 - column, plane, there, :],
+                        halo_sem, (phase, 8 * count + 2 * n + side), at(pair_step, step),
                     ),
                     turn, turns[1 - side][2],
                 )
                 for side, (column, step, turn) in enumerate(turns)
             ])
-            for copy in corners[plane]:
+            for copy in corners[n]:
                 copy.start()
-        beside = [send_sideways(wide, phase, plane, middle, 4 + 2 * plane, False) for plane in range(2)]
+        beside = [send_sideways(wide, phase, plane, middle, 2 * count + 2 * plane, False) for plane in range(2)]
         return direct, corners, beside
 
     def pass_near(wide, phase, state):
         direct, corners, beside = state
         passed = []
-        for plane in range(2):
-            direct[plane].wait_recv()
+        for n, (plane, part) in enumerate(pieces):
+            here, there = piece_rows(near_start, part), piece_rows(far_start, part)
+            direct[n].wait_recv()
             passed.append(Copy(remote(
-                wide.at[1, plane, near, :], wide.at[1, plane, far_rows, :],
-                halo_sem, (phase, 2 + plane), at(pass_step, 0),
+                wide.at[1, plane, here, :], wide.at[1, plane, there, :],
+                halo_sem, (phase, count + n), at(pass_step, 0),
             )))
             passed[-1].start()
-            beside.append(send_sideways(wide, phase, plane, near, 8 + 2 * plane, True))
-        for plane in range(2):
+            beside.append(send_sideways(wide, phase, plane, here, 4 * count + 2 * n, True))
+        for n, (plane, part) in enumerate(pieces):
+            here, there = piece_rows(near_start, part), piece_rows(far_start, part)
             for side, (column, step, turn) in enumerate(turns):
-                corners[plane][1 - side].wait_recv()
+                corners[n][1 - side].wait_recv()
                 passed.append(Copy(
                     remote(
-                        wide.at[column, plane, near, :], wide.at[column, plane, far_rows, :],
-                        halo_sem, (phase, 20 + 2 * plane + side), at(pass_step, 0),
+                        wide.at[column, plane, here, :], wide.at[column, plane, there, :],
+                        halo_sem, (phase, 10 * count + 2 * n + side), at(pass_step, 0),
                     ),
                     turn, turn,
                 ))
@@ -166,18 +175,18 @@
         return passed
 
     def pass_far(wide, phase, state, passed):
-        for plane in range(2):
-            passed[plane].wait_recv()
-            state[2].append(send_sideways(wide, phase, plane, far_rows, 12 + 2 * plane, True))
+        for n, (plane, part) in enumerate(pieces):
+            passed[n].wait_recv()
+            state[2].append(send_sideways(wide, phase, plane, piece_rows(far_start, part), 6 * count + 2 * n, True))
 
     def finish_gather(state, passed):
         direct, corners, beside = state
         for pair in beside:
             for copy in pair:
                 copy.wait()
-        for copy in passed[2:]:
+        for copy in passed[count:]:
             copy.wait_recv()
-        for copy in direct + passed + corners[0] + corners[1]:
+        for copy in direct + passed + [copy for pair in corners for copy in pair]:
             copy.wait_send()
 
     loads[0].wait()
@@ -364,31 +373,47 @@
             copies[-1].start()
         return copies
 
-    energy_copies, scales = [], []
+    energy_copies, scales = [[] for _ in range(ITERS)], []
+
+    def put_results(iteration):
+        for copy in energy_copies[iteration]:
+            copy.wait()
+        step, scale = scales[iteration]
+        steps_out[iteration] = step[0, 0]
+        energy = jnp.sum(jnp.sum(energy_recv[iteration], axis=0), axis=1, keepdims=True) * scale
+        for slot in range(slots):
+            alive = (slot < live_ref[0]).astype(jnp.float32)
+            energies_out[iteration, slot] = energy[slot, 0] * alive
+
     for iteration in range(ITERS):
         for stage in stages:
             for slot in range(slots):
                 stage(slot)
 
-        def gathered(column, plane, start):
+        def gathered(column, plane, start, length):
             summed = None
             for slot in range(slots):
-                term = deposit[slot, column, plane, pl.ds(start + tile - centres_ref[slot, 0], tile), :]
+                term = deposit[slot, column, plane, pl.ds(start + tile - centres_ref[slot, 0], length), :]
                 summed = term if summed is None else summed + term
             return summed
 
         sides, corners = {}, []
+        outer = [(name, *piece) for name in ("far", "near") for piece in pieces]
         starts = {"far": far_start, "near": near_start, "middle": tile}
-        for place, (name, plane) in enumerate((name, plane) for name in starts for plane in range(2)):
-            rows = pl.ds(starts[name], tile)
+        for place, (name, plane, part) in enumerate(outer + [("middle", 0, None), ("middle", 1, None)]):
+            if name == "middle":
+                rows, start, length = middle, tile, tile
+            else:
+                rows, start, length = piece_rows(starts[name], part), starts[name] + part * depth, depth
             pair = []
             for side, (column, step, turn) in enumerate(turns):
-                fold[iteration, column, plane, rows, :] = gathered(column, plane, starts[name])
+                fold[iteration, column, plane, rows, :] = gathered(column, plane, start, length)
                 if name == "far":
                     corners.append(Copy(
                         remote(
-                            fold.at[iteration, column, plane, rows, :], corner_z.at[iteration, side, plane],
-                            fold_sem, (iteration, 16 + 2 * plane + side), at(-pass_step, 0),
+                            fold.at[iteration, column, plane, rows, :],
+                            corner_z.at[iteration, side, plane, piece_rows(0, part), :],
+                            fold_sem, (iteration, 8 * count + 2 * place + side), at(-pass_step, 0),
                         ),
                         turn, turn,
                     ))
@@ -402,14 +427,14 @@
                 )
                 copy.start()
                 pair.append(copy)
-            sides[name, plane] = pair
+            sides[name, plane, part] = pair
         for name in starts:
             for plane in range(2):
-                fold[iteration, 1, plane, pl.ds(starts[name], tile), :] = gathered(1, plane, starts[name])
-
-        def add_sides(name, plane):
-            rows = pl.ds(starts[name], tile)
-            for side, copy in enumerate(sides[name, plane]):
+                fold[iteration, 1, plane, pl.ds(starts[name], tile), :] = gathered(1, plane, starts[name], tile)
+
+        def add_sides(name, plane, part):
+            rows = middle if name == "middle" else piece_rows(starts[name], part)
+            for side, copy in enumerate(sides[name, plane, part]):
                 def add(side=side):
                     fold[iteration, 1, plane, rows, :] += fold_x[iteration, side, plane, rows, :]
 
@@ -417,50 +442,55 @@
                 when(None if name == "middle" else (on_left, on_right)[side], add)
 
         passed_on, folds, straight = [], [], []
-        for plane in range(2):
-            add_sides("far", plane)
+        for n, (plane, part) in enumerate(pieces):
+            add_sides("far", plane, part)
             passed_on.append(remote(
-                fold.at[iteration, 1, plane, far_rows, :], fold_z.at[iteration, plane],
-                fold_sem, (iteration, 12 + plane), at(-pass_step, 0),
+                fold.at[iteration, 1, plane, piece_rows(far_start, part), :],
+                fold_z.at[iteration, plane, piece_rows(0, part), :],
+                fold_sem, (iteration, 6 * count + n), at(-pass_step, 0),
             ))
-            passed_on[plane].start()
-        for plane in range(2):
+            passed_on[n].start()
+        for n, (plane, part) in enumerate(pieces):
+            here, rows = piece_rows(0, part), piece_rows(near_start, part)
             for side, (column, step, turn) in enumerate(turns):
-                def add_corner(plane=plane, side=side, column=column):
-                    fold[iteration, column, plane, near, :] += corner_z[iteration, side, plane]
-
-                corners[2 * plane + side].wait_recv()
+                def add_corner(plane=plane, side=side, column=column, here=here, rows=rows):
+                    fold[iteration, column, plane, rows, :] += corner_z[iteration, side, plane, here, :]
+
+                corners[2 * n + side].wait_recv()
                 when(turn, add_corner)
                 straight.append(Copy(
                     remote(
-                        fold.at[iteration, column, plane, near, :], corner_y.at[iteration, side, plane],
-                        fold_sem, (iteration, 20 + 2 * plane + side), at(pair_step, step),
+                        fold.at[iteration, column, plane, rows, :], corner_y.at[iteration, side, plane, here, :],
+                        fold_sem, (iteration, 10 * count + 2 * n + side), at(pair_step, step),
                     ),
                     turn, turns[1 - side][2],
                 ))
                 straight[-1].start()
+        for n, (plane, part) in enumerate(pieces):
+            here, rows = piece_rows(0, part), piece_rows(near_start, part)
+            add_sides("near", plane, part)
+            passed_on[n].wait_recv()
+            fold[iteration, 1, plane, rows, :] += fold_z[iteration, plane, here, :]
+            folds.append(remote(
+                fold.at[iteration, 1, plane, rows, :], fold_y.at[iteration, plane, here, :],
+                fold_sem, (iteration, 7 * count + n), at(pair_step, 0),
+            ))
+            folds[n].start()
         for plane in range(2):
-            add_sides("near", plane)
-            passed_on[plane].wait_recv()
-            fold[iteration, 1, plane, near, :] += fold_z[iteration, plane]
-            folds.append(remote(
-                fold.at[iteration, 1, plane, near, :], fold_y.at[iteration, plane],
-                fold_sem, (iteration, 14 + plane), at(pair_step, 0),
-            ))
-            folds[plane].start()
-        for plane in range(2):
-            add_sides("middle", plane)
-        for plane in range(2):
+            add_sides("middle", plane, None)
+        for n, (plane, part) in enumerate(pieces):
+            here, rows = piece_rows(0, part), piece_rows(tile, part)
             for side in range(2):
-                def add_straight(plane=plane, side=side):
-                    fold[iteration, 1, plane, middle, :] += corner_y[iteration, side, plane]
-
-                straight[2 * plane + side].wait_recv()
+                def add_straight(plane=plane, side=side, here=here, rows=rows):
+                    fold[iteration, 1, plane, rows, :] += corner_y[iteration, side, plane, here, :]
+
+                straight[2 * n + side].wait_recv()
                 when(turns[1 - side][2], add_straight)
         cover = coverage[...]
         gradient, moved = [], []
         for plane in range(2):
-            folds[plane].wait_recv()
+            for part in range(PARTS):
+                folds[plane * PARTS + part].wait_recv()
             gradient.append(fold[iteration, 1, plane, middle, :] + fold_y[iteration, plane])
             moved.append(gradient[plane] / (cover + 0.5))
             direction_ext[iteration, 1, plane, middle, :] = moved[plane]
@@ -489,7 +519,10 @@
                     energy_sem, (iteration, n), at(k, c),
                 )
                 copy.start()
-                energy_copies.append(copy)
+                energy_copies[iteration].append(copy)
+        if last:
+            for earlier in range(iteration):
+                put_results(earlier)
         for copy in first_sums:
             copy.wait()
         sums_y[iteration, my_obj] = jnp.sum(sums_x[iteration], axis=0)
@@ -514,15 +547,7 @@
             object_out[...] = (
                 extended[1, :, middle, :] + step.reshape(1, 1, 1) * direction_ext[iteration, 1, :, middle, :]
             )
-    for copy in energy_copies:
-        copy.wait()
-    for iteration in range(ITERS):
-        step, scale = scales[iteration]
-        steps_out[iteration] = step[0, 0]
-        energy = jnp.sum(jnp.sum(energy_recv[iteration], axis=0), axis=1, keepdims=True) * scale
-        for slot in range(slots):
-            alive = (slot < live_ref[0]).astype(jnp.float32)
-            energies_out[iteration, slot] = energy[slot, 0] * alive
+    put_results(ITERS - 1)
 
 
 def on_device(n_scan, n_obj, object_field, probe_modes, patterns, gain_map, defect_mask, probe_centres, live_counts):
@@ -577,8 +602,8 @@
             pltpu.VMEM((ITERS, n_obj, 8, tile), f32),
             pltpu.SemaphoreType.DMA((8,)),
             pltpu.SemaphoreType.DMA((2, 9)),
-            pltpu.SemaphoreType.DMA((2, ITERS, 24)),
-            pltpu.SemaphoreType.DMA((2, ITERS, 24)),
+            pltpu.SemaphoreType.DMA((2, ITERS, 24 * PARTS)),
+            pltpu.SemaphoreType.DMA((2, ITERS, 24 * PARTS)),
             pltpu.SemaphoreType.DMA((2, ITERS, 9)),
             pltpu.SemaphoreType.DMA((2, ITERS, n_scan + n_obj)),
         ],

time: 84.1 us -> 82.6 us (0.982)
  Pallas kernels: 80.2 us -> 78.7 us
    pallas_call x1, Pallas kernels: 80.2 us -> 78.7 us  [on_device(): pl.pallas_call(functools.partial(kernel, n_scan, n_obj), out_shape=(jax.S...]
where the time goes in v6:
time: 82.6 us; the launch traced here: 82.4 us
  Pallas kernels  78.7 us (95%)
  local copies, waits for them, and re-layouts  2.4 us (3%)
  between operations  1.3 us (2%)
    pallas_call x1, Pallas kernels, on_device(): pl.pallas_call(functools.partial(kernel, n_scan, n_obj), out_shape=(jax.S...  78.7 us
    unnamed x5, local copies, waits for them, and re-layouts  2.4 us

profile of v6, /device:TPU:1, one launch (start us, length us, event | category | flops | bytes accessed | tf_op | source)
XLA Modules:
  0.0 82.4 jit_solution(4853648622230481891)
XLA Ops:
  1.3 0.0 copy-start
  1.3 0.7 copy-done
  2.0 78.7 %shard_map.103 = (f32[2,128,128]{2,1,0:T(8,128)S(1)}, f32[2]{0:T(128)S(1)}, f32[2,2]{1,0:T(2,128)S(1)}) custom-call(f32[2,128,128]{2,1,0:T(8,128)} %object_hbm.1, f32[4,256,512]{2,1,0:T(8,128)} %probe_hbm.1, bf16[2,256,256]{2,1,0:T(8,128)(2,1)} %patterns_hbm.1, f32[256,256]{1,0:T(8,128)} %gain_hbm.1, s32[256,256]{1,0:T(8,128)} %mask_hbm.1, ...), custom_call_target="tpu_custom_call" | custom-call | flops 4294967296 | bytes 8388608 | tf_op jit(solution)/shard_map/pallas_call | solution.py:563
  80.7 0.7 copy.15
  81.4 0.5 copy.16
  81.9 0.6 copy.17
Async XLA Ops:
  1.3 0.7 copy-start

commit v7 on v6

--- a/solution.py
+++ b/solution.py
@@ -35,7 +35,7 @@
     object_hbm, probe_hbm, patterns_hbm, gain_hbm, mask_hbm, table_hbm, centres_hbm, live_hbm,
     object_out, steps_out, energies_out,
     probe_ref, patterns_ref, gain_ref, mask_ref, table_ref, centres_ref, live_ref,
-    info, extended, direction_ext, amplitude, power_pad, shifted, coverage, patch, waves, stacked, far, update,
+    info, extended, direction_ext, amplitude, power_pad, shifted, coverage, patch, waves, stacked, far,
     deposit, fold, fold_x, fold_y, fold_z, corner_y, corner_z, energy_send, energy_recv, sums_x, sums_y,
     load_sem, info_sem, halo_sem, fold_sem, energy_sem, sums_sem,
 ):
@@ -66,14 +66,13 @@
     loads = [
         pltpu.make_async_copy(source, target, load_sem.at[n]) for n, (source, target) in enumerate(pairs)
     ]
-    for load in loads:
-        load.start()
-
     partners = [(0, c) for c in range(1, n_scan)] + [(k, 0) for k in range(1, n_obj)]
     partners += [(k, c) for k, c in AROUND if k and c]
     barrier = pltpu.get_barrier_semaphore()
     for k, c in partners:
         pl.semaphore_signal(barrier, inc=1, device_id=at(k, c), device_id_type=MESH)
+    for load in loads:
+        load.start()
     pl.semaphore_wait(barrier, len(partners))
 
     odd = lax.rem(my_obj, 2)
@@ -183,11 +182,10 @@
         direct, corners, beside = state
         for pair in beside:
             for copy in pair:
-                copy.wait()
+                copy.wait_recv()
         for copy in passed[count:]:
             copy.wait_recv()
-        for copy in direct + passed + [copy for pair in corners for copy in pair]:
-            copy.wait_send()
+        return direct + passed + [copy for pair in corners + beside for copy in pair]
 
     loads[0].wait()
     state = start_gather(extended, 0)
@@ -261,7 +259,7 @@
             shifted[n, slot] = moved
             total = total + moved * alive
     coverage[...] = total
-    finish_gather(state, passed)
+    sent = finish_gather(state, passed)
 
     wide_lane = lax.broadcasted_iota(jnp.int32, (size, tile), 1)
 
@@ -327,36 +325,33 @@
                     waves[slot, mode, rows, parity * size : parity * size + tile] = value[:tile, lanes]
                     waves[slot, mode, rows, parity * size + tile : (parity + 1) * size] = value[tile:, lanes]
 
-    def back_along_columns(slot):
-        for plane in range(2):
-            for half in range(2):
-                lanes = slice(half * tile, (half + 1) * tile)
-                update[slot, plane, :, lanes] = -power_pad[half, tile : tile + size, :] * patch[slot, plane, :, lanes]
-        for mode in range(modes):
-            even = product(waves[slot, mode, :, :size], table_ref[2])
-            odd = product(waves[slot, mode, :, size:], table_ref[3])
-            for half, wave in enumerate((even + odd, even - odd)):
-                real, imag = wave[:, :tile], wave[:, tile:]
-                lanes = slice(half * tile, (half + 1) * tile)
-                probe_real = probe_ref[mode, :, lanes]
-                probe_imag = probe_ref[mode, :, size + half * tile : size + (half + 1) * tile]
-                update[slot, 0, :, lanes] += real * probe_real + imag * probe_imag
-                update[slot, 1, :, lanes] += imag * probe_real - real * probe_imag
-
-    def put_deposit(slot):
+    def back_along_columns(slot, start):
+        rows = pl.ds(pl.multiple_of(start, tile), tile)
+        placed_rows = pl.ds(pl.multiple_of(start + tile, tile), tile)
+        even = product(waves[slot, :, rows, :size].reshape(modes * tile, size), table_ref[2])
+        odd_part = product(waves[slot, :, rows, size:].reshape(modes * tile, size), table_ref[3])
+        updates = []
+        for half, wave in enumerate((even + odd_part, even - odd_part)):
+            lanes = slice(half * tile, (half + 1) * tile)
+            power = power_pad[half, placed_rows, :]
+            real_sum, imag_sum = (-power * patch[slot, plane, rows, lanes] for plane in range(2))
+            for mode in range(modes):
+                real, imag = wave[mode * tile : (mode + 1) * tile, :tile], wave[mode * tile : (mode + 1) * tile, tile:]
+                probe_real = probe_ref[mode, rows, lanes]
+                probe_imag = probe_ref[mode, rows, size + half * tile : size + (half + 1) * tile]
+                real_sum = real_sum + (real * probe_real + imag * probe_imag)
+                imag_sum = imag_sum + (imag * probe_real - real * probe_imag)
+            updates.append((real_sum, imag_sum))
         column = centres_ref[slot, 1]
         alive = jnp.where(slot < live_ref[0], 1.0, 0.0)
-        before = wide_lane < column
+        before = lane < column
         for plane in range(2):
-            low = pltpu.roll(update[slot, plane, :, :tile] * alive, column, 1)
-            high = pltpu.roll(update[slot, plane, :, tile:] * alive, column, 1)
-            deposit[slot, 0, plane, tile : tile + size, :] = jnp.where(before, 0.0, low)
-            deposit[slot, 1, plane, tile : tile + size, :] = jnp.where(before, low, high)
-            deposit[slot, 2, plane, tile : tile + size, :] = jnp.where(before, high, 0.0)
-
-    stages = (
-        take_patch, exit_waves, along_columns, along_rows, revise, back_along_rows, back_along_columns, put_deposit
-    )
+            low, high = (pltpu.roll(updates[half][plane] * alive, column, 1) for half in range(2))
+            deposit[slot, 0, plane, placed_rows, :] = jnp.where(before, 0.0, low)
+            deposit[slot, 1, plane, placed_rows, :] = jnp.where(before, low, high)
+            deposit[slot, 2, plane, placed_rows, :] = jnp.where(before, high, 0.0)
+
+    stages = (take_patch, exit_waves, along_columns, along_rows, revise, back_along_rows)
 
     row_id = lax.broadcasted_iota(jnp.int32, (8, tile), 0)
 
@@ -389,6 +384,8 @@
         for stage in stages:
             for slot in range(slots):
                 stage(slot)
+        for slot in range(slots):
+            back_along_columns(slot, tile * odd)
 
         def gathered(column, plane, start, length):
             summed = None
@@ -400,7 +397,9 @@
         sides, corners = {}, []
         outer = [(name, *piece) for name in ("far", "near") for piece in pieces]
         starts = {"far": far_start, "near": near_start, "middle": tile}
-        for place, (name, plane, part) in enumerate(outer + [("middle", 0, None), ("middle", 1, None)]):
+        order = [(place, *entry) for place, entry in enumerate(outer + [("middle", 0, None), ("middle", 1, None)])]
+
+        def send_out(place, name, plane, part):
             if name == "middle":
                 rows, start, length = middle, tile, tile
             else:
@@ -428,6 +427,13 @@
                 copy.start()
                 pair.append(copy)
             sides[name, plane, part] = pair
+
+        for entry in order[:count]:
+            send_out(*entry)
+        for slot in range(slots):
+            back_along_columns(slot, tile * (1 - odd))
+        for entry in order[count:]:
+            send_out(*entry)
         for name in starts:
             for plane in range(2):
                 fold[iteration, 1, plane, pl.ds(starts[name], tile), :] = gathered(1, plane, starts[name], tile)
@@ -529,9 +535,8 @@
         second_sums = sum_start(sums_y, my_obj, n_scan, n_obj, lambda other: at(other, 0), iteration)
         if not last:
             pass_far(direction_ext.at[iteration], 1 + iteration, state, passed)
-        for pair in sides.values():
-            for copy in pair:
-                copy.wait_send()
+        for copy in sent + [copy for pair in sides.values() for copy in pair]:
+            copy.wait_send()
         for copy in folds + passed_on + corners + straight:
             copy.wait_send()
         for copy in second_sums:
@@ -541,7 +546,7 @@
         step = rows[0:1] / rows[1:2]
         scales.append((step, rows[2:3] * (1.0 / tile) / rows[1:2]))
         if not last:
-            finish_gather(state, passed)
+            sent = finish_gather(state, passed)
             extended[...] = extended[...] + step.reshape(1, 1, 1, 1) * direction_ext[iteration]
         else:
             object_out[...] = (
@@ -588,7 +593,6 @@
             pltpu.VMEM((slots, modes, size, 2 * size), jnp.bfloat16),
             pltpu.VMEM((slots, modes, 2 * size, size), jnp.bfloat16),
             pltpu.VMEM((slots, modes, 2 * size, size), f32),
-            pltpu.VMEM((slots, 2, size, size), f32),
             pltpu.VMEM((slots, 3, 2, size + 2 * tile, tile), f32),
             pltpu.VMEM((ITERS, 3, 2, extent, tile), f32),
             pltpu.VMEM((ITERS, 2, 2, extent, tile), f32),

time: 82.6 us -> 81.1 us (0.982)
  Pallas kernels: 78.7 us -> 77.2 us
    pallas_call x1, Pallas kernels: 78.7 us -> 77.2 us  [on_device(): pl.pallas_call(functools.partial(kernel, n_scan, n_obj), out_shape=(jax.S...]
where the time goes in v7:
time: 81.1 us; the launch traced here: 80.9 us
  Pallas kernels  77.2 us (95%)
  local copies, waits for them, and re-layouts  2.4 us (3%)
  between operations  1.3 us (2%)
    pallas_call x1, Pallas kernels, on_device(): pl.pallas_call(functools.partial(kernel, n_scan, n_obj), out_shape=(jax.S...  77.2 us
    unnamed x5, local copies, waits for them, and re-layouts  2.4 us

profile of v7, /device:TPU:1, one launch (start us, length us, event | category | flops | bytes accessed | tf_op | source)
XLA Modules:
  0.0 80.9 jit_solution(6326494524845329048)
XLA Ops:
  1.3 0.0 copy-start
  1.3 0.7 copy-done
  2.0 77.2 %shard_map.103 = (f32[2,128,128]{2,1,0:T(8,128)S(1)}, f32[2]{0:T(128)S(1)}, f32[2,2]{1,0:T(2,128)S(1)}) custom-call(f32[2,128,128]{2,1,0:T(8,128)} %object_hbm.1, f32[4,256,512]{2,1,0:T(8,128)} %probe_hbm.1, bf16[2,256,256]{2,1,0:T(8,128)(2,1)} %patterns_hbm.1, f32[256,256]{1,0:T(8,128)} %gain_hbm.1, s32[256,256]{1,0:T(8,128)} %mask_hbm.1, ...), custom_call_target="tpu_custom_call" | custom-call | flops 4294967296 | bytes 8388608 | tf_op jit(solution)/shard_map/pallas_call | solution.py:568
  79.2 0.7 copy.15
  79.8 0.5 copy.16
  80.4 0.6 copy.17
Async XLA Ops:
  1.3 0.7 copy-start

commit v8 on v7

--- a/solution.py
+++ b/solution.py
@@ -66,11 +66,16 @@
     loads = [
         pltpu.make_async_copy(source, target, load_sem.at[n]) for n, (source, target) in enumerate(pairs)
     ]
-    partners = [(0, c) for c in range(1, n_scan)] + [(k, 0) for k in range(1, n_obj)]
-    partners += [(k, c) for k, c in AROUND if k and c]
+    run = n_scan // 2
+    my_run, my_place = my_scan // run, lax.rem(my_scan, run)
+    in_run = [
+        {"scan": my_run * run + lax.rem(my_place + other, run), "obj": my_obj} for other in range(1, run)
+    ]
+    across = [at(k, c) for c in (0, run) for k in range(n_obj) if k or c]
+    partners = in_run + across + [at(0, -1), at(0, 1)] + [at(k, c) for k, c in AROUND if k and c]
     barrier = pltpu.get_barrier_semaphore()
-    for k, c in partners:
-        pl.semaphore_signal(barrier, inc=1, device_id=at(k, c), device_id_type=MESH)
+    for partner in partners:
+        pl.semaphore_signal(barrier, inc=1, device_id=partner, device_id_type=MESH)
     for load in loads:
         load.start()
     pl.semaphore_wait(barrier, len(partners))
@@ -81,8 +86,7 @@
     near, far_rows = pl.ds(near_start, tile), pl.ds(far_start, tile)
     pair_step, pass_step = 1 - 2 * odd, 2 - 4 * odd
 
-    run = n_scan // 2
-    turn_right, turn_left = lax.rem(my_scan, run) == run - 1, lax.rem(my_scan, run) == 0
+    turn_right, turn_left = my_place == run - 1, my_place == 0
     on_right, on_left = jnp.logical_not(turn_right), jnp.logical_not(turn_left)
     turns = ((2, 1, turn_right), (0, -1, turn_left))
 
@@ -360,13 +364,18 @@
 
     live_number = live_ref[0].astype(jnp.float32)
 
-    def sum_start(table, mine, base, count, where, iteration):
+    def sum_start(table, mine, base, devices, iteration):
         copies = []
-        for other in range(1, count):
+        for n, device in enumerate(devices):
             block = table.at[iteration, mine]
-            copies.append(remote(block, block, sums_sem, (iteration, base + other), where(other)))
+            copies.append(remote(block, block, sums_sem, (iteration, base + n), device))
             copies[-1].start()
         return copies
+
+    lane_id = lax.broadcasted_iota(jnp.int32, (1, tile), 1)
+
+    def whole(value):
+        return jnp.sum(jnp.sum(value, axis=0, keepdims=True), axis=1, keepdims=True)
 
     energy_copies, scales = [[] for _ in range(ITERS)], []
 
@@ -505,11 +514,12 @@
             state = start_gather(direction_ext.at[iteration], 1 + iteration)
 
         squares = moved[0] * moved[0] + moved[1] * moved[1]
-        sums_x[iteration, my_scan] = (
-            as_row(moved[0] * gradient[0] + moved[1] * gradient[1], 0)
-            + as_row(cover * squares, 1) + jnp.where(row_id == 2, live_number, 0.0)
+        numerator = whole(moved[0] * gradient[0] + moved[1] * gradient[1])
+        denominator = whole(cover * squares)
+        sums_x[iteration, my_place] = jnp.where(
+            lane_id == 0, numerator, jnp.where(lane_id == 1, denominator, jnp.where(lane_id == 2, live_number, 0.0))
         )
-        first_sums = sum_start(sums_x, my_scan, 0, n_scan, lambda other: at(0, other), iteration)
+        first_sums = sum_start(sums_x, my_place, 0, in_run, iteration)
         if not last:
             passed = pass_near(direction_ext.at[iteration], 1 + iteration, state)
         for n, (k, c) in enumerate(AROUND):
@@ -531,8 +541,9 @@
                 put_results(earlier)
         for copy in first_sums:
             copy.wait()
-        sums_y[iteration, my_obj] = jnp.sum(sums_x[iteration], axis=0)
-        second_sums = sum_start(sums_y, my_obj, n_scan, n_obj, lambda other: at(other, 0), iteration)
+        mine = my_run * n_obj + my_obj
+        sums_y[iteration, mine] = jnp.sum(sums_x[iteration], axis=0)
+        second_sums = sum_start(sums_y, mine, run, across, iteration)
         if not last:
             pass_far(direction_ext.at[iteration], 1 + iteration, state, passed)
         for copy in sent + [copy for pair in sides.values() for copy in pair]:
@@ -542,9 +553,9 @@
         for copy in second_sums:
             copy.wait()
         everywhere = jnp.sum(sums_y[iteration], axis=0)
-        rows = jnp.sum(everywhere, axis=1, keepdims=True)
-        step = rows[0:1] / rows[1:2]
-        scales.append((step, rows[2:3] * (1.0 / tile) / rows[1:2]))
+        numerator, denominator, live_total = (everywhere[:, n : n + 1] for n in range(3))
+        step = numerator / denominator
+        scales.append((step, live_total / denominator))
         if not last:
             sent = finish_gather(state, passed)
             extended[...] = extended[...] + step.reshape(1, 1, 1, 1) * direction_ext[iteration]
@@ -602,14 +613,14 @@
             pltpu.VMEM((ITERS, 2, 2, tile, tile), f32),
             pltpu.VMEM((ITERS, 9, 8, tile), f32),
             pltpu.VMEM((ITERS, 9, 8, tile), f32),
-            pltpu.VMEM((ITERS, n_scan, 8, tile), f32),
-            pltpu.VMEM((ITERS, n_obj, 8, tile), f32),
+            pltpu.VMEM((ITERS, n_scan // 2, 1, tile), f32),
+            pltpu.VMEM((ITERS, 2 * n_obj, 1, tile), f32),
             pltpu.SemaphoreType.DMA((8,)),
             pltpu.SemaphoreType.DMA((2, 9)),
             pltpu.SemaphoreType.DMA((2, ITERS, 24 * PARTS)),
             pltpu.SemaphoreType.DMA((2, ITERS, 24 * PARTS)),
             pltpu.SemaphoreType.DMA((2, ITERS, 9)),
-            pltpu.SemaphoreType.DMA((2, ITERS, n_scan + n_obj)),
+            pltpu.SemaphoreType.DMA((2, ITERS, n_scan // 2 + 2 * n_obj)),
         ],
         compiler_params=pltpu.CompilerParams(
             collective_id=0, has_side_effects=True, vmem_limit_bytes=55000 * 1024

time: 81.1 us -> 79.7 us (0.983)
  Pallas kernels: 77.2 us -> 75.9 us
    pallas_call x1, Pallas kernels: 77.2 us -> 75.9 us  [on_device(): pl.pallas_call(functools.partial(kernel, n_scan, n_obj), out_shape=(jax.S...]
where the time goes in v8:
time: 79.7 us; the launch traced here: 79.6 us
  Pallas kernels  75.9 us (95%)
  local copies, waits for them, and re-layouts  2.4 us (3%)
  between operations  1.3 us (2%)
    pallas_call x1, Pallas kernels, on_device(): pl.pallas_call(functools.partial(kernel, n_scan, n_obj), out_shape=(jax.S...  75.9 us
    unnamed x5, local copies, waits for them, and re-layouts  2.4 us

profile of v8, /device:TPU:1, one launch (start us, length us, event | category | flops | bytes accessed | tf_op | source)
XLA Modules:
  0.0 79.6 jit_solution(18160368122869567977)
XLA Ops:
  1.3 0.0 copy-start
  1.3 0.7 copy-done
  2.0 75.9 %shard_map.103 = (f32[2,128,128]{2,1,0:T(8,128)S(1)}, f32[2]{0:T(128)S(1)}, f32[2,2]{1,0:T(2,128)S(1)}) custom-call(f32[2,128,128]{2,1,0:T(8,128)} %object_hbm.1, f32[4,256,512]{2,1,0:T(8,128)} %probe_hbm.1, bf16[2,256,256]{2,1,0:T(8,128)(2,1)} %patterns_hbm.1, f32[256,256]{1,0:T(8,128)} %gain_hbm.1, s32[256,256]{1,0:T(8,128)} %mask_hbm.1, ...), custom_call_target="tpu_custom_call" | custom-call | flops 4294967296 | bytes 8388608 | tf_op jit(solution)/shard_map/pallas_call | solution.py:579
  77.8 0.7 copy.15
  78.5 0.5 copy.16
  79.0 0.6 copy.17
Async XLA Ops:
  1.3 0.7 copy-start

commit v9 on v8

--- a/solution.py
+++ b/solution.py
@@ -379,15 +379,12 @@
 
     energy_copies, scales = [[] for _ in range(ITERS)], []
 
-    def put_results(iteration):
+    def raw_energies(iteration):
         for copy in energy_copies[iteration]:
             copy.wait()
-        step, scale = scales[iteration]
-        steps_out[iteration] = step[0, 0]
-        energy = jnp.sum(jnp.sum(energy_recv[iteration], axis=0), axis=1, keepdims=True) * scale
-        for slot in range(slots):
-            alive = (slot < live_ref[0]).astype(jnp.float32)
-            energies_out[iteration, slot] = energy[slot, 0] * alive
+        total = jnp.sum(jnp.sum(energy_recv[iteration], axis=0), axis=1, keepdims=True)
+        in_row = jnp.sum(jnp.where(row_id == lane[:8], total, 0.0), axis=0, keepdims=True)
+        return jnp.where(lane_id < live_ref[0], in_row, 0.0)
 
     for iteration in range(ITERS):
         for stage in stages:
@@ -536,9 +533,6 @@
                 )
                 copy.start()
                 energy_copies[iteration].append(copy)
-        if last:
-            for earlier in range(iteration):
-                put_results(earlier)
         for copy in first_sums:
             copy.wait()
         mine = my_run * n_obj + my_obj
@@ -550,6 +544,8 @@
             copy.wait_send()
         for copy in folds + passed_on + corners + straight:
             copy.wait_send()
+        if last:
+            raw = [raw_energies(each) for each in range(ITERS)]
         for copy in second_sums:
             copy.wait()
         everywhere = jnp.sum(sums_y[iteration], axis=0)
@@ -563,7 +559,12 @@
             object_out[...] = (
                 extended[1, :, middle, :] + step.reshape(1, 1, 1) * direction_ext[iteration, 1, :, middle, :]
             )
-    put_results(ITERS - 1)
+    step_row = jnp.zeros((1, tile), jnp.float32)
+    for iteration in range(ITERS):
+        step, scale = scales[iteration]
+        step_row = jnp.where(lane_id == iteration, step, step_row)
+        energies_out[iteration : iteration + 1, :] = (raw[iteration] * scale)[:, :slots]
+    steps_out[...] = step_row[0, :ITERS]
 
 
 def on_device(n_scan, n_obj, object_field, probe_modes, patterns, gain_map, defect_mask, probe_centres, live_counts):
@@ -573,7 +574,7 @@
     extent = tile + size
     table = transform_tables(size)
     f32 = jnp.float32
-    vmem, smem = pl.BlockSpec(memory_space=pltpu.VMEM), pl.BlockSpec(memory_space=pltpu.SMEM)
+    vmem = pl.BlockSpec(memory_space=pltpu.VMEM)
     hbm = pl.BlockSpec(memory_space=pltpu.HBM)
     flops = ITERS * slots * modes * 4 * 2 * (2 * size) * size * size
     outputs = pl.pallas_call(
@@ -584,7 +585,7 @@
             jax.ShapeDtypeStruct((ITERS, slots), f32),
         ),
         in_specs=[hbm] * 8,
-        out_specs=(vmem, smem, smem),
+        out_specs=(vmem, vmem, vmem),
         scratch_shapes=[
             pltpu.VMEM(probe_modes.shape, f32),
             pltpu.VMEM(patterns.shape, patterns.dtype),

time: 79.7 us -> 78.9 us (0.990)
  Pallas kernels: 75.9 us -> 75.1 us
    pallas_call x1, Pallas kernels: 75.9 us -> 75.1 us  [on_device(): pl.pallas_call(functools.partial(kernel, n_scan, n_obj), out_shape=(jax.S...]
where the time goes in v9:
time: 78.9 us; the launch traced here: 78.8 us
  Pallas kernels  75.1 us (95%)
  local copies, waits for them, and re-layouts  2.4 us (3%)
  between operations  1.3 us (2%)
    pallas_call x1, Pallas kernels, on_device(): pl.pallas_call(functools.partial(kernel, n_scan, n_obj), out_shape=(jax.S...  75.1 us
    unnamed x5, local copies, waits for them, and re-layouts  2.4 us

profile of v9, /device:TPU:1, one launch (start us, length us, event | category | flops | bytes accessed | tf_op | source)
XLA Modules:
  0.0 78.8 jit_solution(13503866500467325285)
XLA Ops:
  1.3 0.0 copy-start
  1.3 0.7 copy-done
  2.0 75.1 %shard_map.103 = (f32[2,128,128]{2,1,0:T(8,128)S(1)}, f32[2]{0:T(128)S(1)}, f32[2,2]{1,0:T(2,128)S(1)}) custom-call(f32[2,128,128]{2,1,0:T(8,128)} %object_hbm.1, f32[4,256,512]{2,1,0:T(8,128)} %probe_hbm.1, bf16[2,256,256]{2,1,0:T(8,128)(2,1)} %patterns_hbm.1, f32[256,256]{1,0:T(8,128)} %gain_hbm.1, s32[256,256]{1,0:T(8,128)} %mask_hbm.1, ...), custom_call_target="tpu_custom_call" | custom-call | flops 4294967296 | bytes 8388608 | tf_op jit(solution)/shard_map/pallas_call | solution.py:580
  77.0 0.7 copy.15
  77.7 0.5 copy.16
  78.2 0.6 copy.17
Async XLA Ops:
  1.3 0.7 copy-start

commit v10 on v9

--- a/solution.py
+++ b/solution.py
@@ -382,8 +382,8 @@
     def raw_energies(iteration):
         for copy in energy_copies[iteration]:
             copy.wait()
-        total = jnp.sum(jnp.sum(energy_recv[iteration], axis=0), axis=1, keepdims=True)
-        in_row = jnp.sum(jnp.where(row_id == lane[:8], total, 0.0), axis=0, keepdims=True)
+        total = jnp.sum(jnp.sum(energy_recv[iteration, :, :slots, :], axis=0), axis=1, keepdims=True)
+        in_row = jnp.sum(jnp.where(row_id[:slots] == lane[:slots], total, 0.0), axis=0, keepdims=True)
         return jnp.where(lane_id < live_ref[0], in_row, 0.0)
 
     for iteration in range(ITERS):
@@ -528,7 +528,7 @@
             else:
                 energy_send[iteration, n] = block
                 copy = remote(
-                    energy_send.at[iteration, n], energy_recv.at[iteration, n],
+                    energy_send.at[iteration, n, :slots, :], energy_recv.at[iteration, n, :slots, :],
                     energy_sem, (iteration, n), at(k, c),
                 )
                 copy.start()

time: 78.9 us -> 78.9 us (level)
  no operation moved by 1% of the time
where the time goes in v10:
time: 78.9 us; the launch traced here: 78.7 us
  Pallas kernels  75 us (95%)
  local copies, waits for them, and re-layouts  2.4 us (3%)
  between operations  1.3 us (2%)
    pallas_call x1, Pallas kernels, on_device(): pl.pallas_call(functools.partial(kernel, n_scan, n_obj), out_shape=(jax.S...  75 us
    unnamed x5, local copies, waits for them, and re-layouts  2.4 us

profile of v10, /device:TPU:1, one launch (start us, length us, event | category | flops | bytes accessed | tf_op | source)
XLA Modules:
  0.0 78.7 jit_solution(14536865683427109786)
XLA Ops:
  1.3 0.0 copy-start
  1.3 0.7 copy-done
  2.0 75.0 %shard_map.103 = (f32[2,128,128]{2,1,0:T(8,128)S(1)}, f32[2]{0:T(128)S(1)}, f32[2,2]{1,0:T(2,128)S(1)}) custom-call(f32[2,128,128]{2,1,0:T(8,128)} %object_hbm.1, f32[4,256,512]{2,1,0:T(8,128)} %probe_hbm.1, bf16[2,256,256]{2,1,0:T(8,128)(2,1)} %patterns_hbm.1, f32[256,256]{1,0:T(8,128)} %gain_hbm.1, s32[256,256]{1,0:T(8,128)} %mask_hbm.1, ...), custom_call_target="tpu_custom_call" | custom-call | flops 4294967296 | bytes 8388608 | tf_op jit(solution)/shard_map/pallas_call | solution.py:580
  76.9 0.7 copy.15
  77.6 0.5 copy.16
  78.1 0.6 copy.17
Async XLA Ops:
  1.3 0.7 copy-start
